TPU v7x, 256 devices: a whole 4x4x8 slice. The times are simulated.
256 devices in a mesh: win: 8 (over y, core), pair: 32 (over x, z).
Axes of the slice: x: 4, y: 4, z: 8, core: 2. Of those that a mesh axis runs over, the one named last changes fastest.
Arguments:
- spectra: bfloat16 [8, 1024, 2, 8192], P('win', 'pair'), may hold values from -130 to 130
- availability: int32 [8, 1024], P('win', 'pair'), may hold values from 0 to 1
- owners: int32 [32, 32], replicated, may hold values from 0 to 1023, as said below
Outputs:
- correlations: float32 [16, 512, 512], P('win', 'pair')
Inputs may be any that keep to these rules, and one draw needn't show every extreme that they name: `owners`: entries are station numbers below 1024; the 32 stations of a row are distinct; a row takes at most 2 stations from one block of 32 stations (stations s with equal s // 32), and exactly 2 from at least one block.
All inputs are finite; a program needn't handle non-finite values.
Results may differ from a plain program's by a relative error of at most 0.0085.
Values may be sent and summed in bfloat16 or wider, within the bound.
A program may use at most 64 MiB of HBM per device.

v0:
```python
import math

import jax
import jax.numpy as jnp
from jax import lax
from jax.sharding import PartitionSpec as P

WB = 64
LAGS = 512
PR = 16
PC = 16
NEED = 32


EPSILON = 1e-06


def whiten(spectra, availability):
    values = spectra.astype(jnp.float32)
    magnitude = jnp.sqrt(
        values[..., 0, :] * values[..., 0, :] + values[..., 1, :] * values[..., 1, :]
    )
    bin_total = magnitude.shape[-1]
    banded = magnitude.reshape(magnitude.shape[:-1] + (bin_total // WB, WB))
    band_level = jnp.mean(banded, axis=-1) + EPSILON
    factor = availability.astype(jnp.float32)[..., None] / band_level
    factor = jnp.repeat(factor, WB, axis=-1)
    return (values * factor[..., None, :]).astype(jnp.bfloat16)


def lag_table(first_bin, bin_width, bin_count, lag_count):
    period = 2 * bin_count
    bin_index = first_bin + lax.iota(jnp.int32, bin_width)
    lag_offset = (lax.iota(jnp.int32, lag_count) - lag_count // 2) % period
    phase_index = bin_index[:, None] * lag_offset[None, :] % period
    angles = phase_index.astype(jnp.float32) * (2.0 * math.pi / period)
    weight = jnp.where(bin_index == 0, 1.0, 2.0).astype(jnp.float32)[:, None] / math.sqrt(period)
    return jnp.concatenate([weight * jnp.cos(angles), -weight * jnp.sin(angles)], axis=0).astype(
        jnp.bfloat16
    )


def cross_spectra(row_spec, col_spec):
    real_part = jnp.einsum(
        "wrf,wcf->crf", row_spec[:, :, 0], col_spec[:, :, 0], preferred_element_type=jnp.float32
    )
    real_part = real_part + jnp.einsum(
        "wrf,wcf->crf", row_spec[:, :, 1], col_spec[:, :, 1], preferred_element_type=jnp.float32
    )
    imag_part = jnp.einsum(
        "wrf,wcf->crf", row_spec[:, :, 1], col_spec[:, :, 0], preferred_element_type=jnp.float32
    )
    imag_part = imag_part - jnp.einsum(
        "wrf,wcf->crf", row_spec[:, :, 0], col_spec[:, :, 1], preferred_element_type=jnp.float32
    )
    return jnp.stack([real_part, imag_part], axis=2)


def split_three(values):
    upper = values.astype(jnp.bfloat16)
    rest = values - upper.astype(jnp.float32)
    middle = rest.astype(jnp.bfloat16)
    lower = (rest - middle.astype(jnp.float32)).astype(jnp.bfloat16)
    return jnp.concatenate([upper, middle, lower], axis=0)


def per_device(spectra, availability, owners):
    n_pair = lax.axis_size("pair")
    n_win = lax.axis_size("win")
    own_index = lax.axis_index("pair")
    win_index = lax.axis_index("win")
    window_count = spectra.shape[0]
    block_size = spectra.shape[1]
    bin_count = spectra.shape[3]
    lag_count = LAGS
    slot_count = max(2, 2 * NEED // n_pair)
    col_share = PC // n_win
    bin_width = min(bin_count, 1024)
    block_count = bin_count // bin_width
    mask_table = lax.all_gather(availability, "win", axis=0, tiled=True)
    whitened = whiten(spectra, availability)
    source = owners // block_size
    station = owners % block_size
    same_source = source[:, :, None] == source[:, None, :]
    earlier = lax.iota(jnp.int32, NEED)[None, :] < lax.iota(jnp.int32, NEED)[:, None]
    slot_rank = jnp.sum(jnp.logical_and(same_source, earlier[None]).astype(jnp.int32), axis=-1)
    picked = jnp.logical_and(
        (source == own_index)[:, None, :],
        slot_rank[:, None, :] == lax.iota(jnp.int32, slot_count)[None, :, None],
    )
    local_station = jnp.sum(picked.astype(jnp.int32) * station[:, None, :], axis=-1).reshape(-1)
    outgoing = jnp.take(whitened, local_station, axis=1).reshape(
        window_count, n_pair, slot_count, 2, bin_count
    )
    outgoing_masks = (
        jnp.take(mask_table, local_station, axis=1)
        .reshape(mask_table.shape[0], n_pair, slot_count)
        .astype(jnp.bfloat16)
    )
    incoming, incoming_masks = (
        lax.all_to_all(outgoing, "pair", split_axis=1, concat_axis=1, tiled=True),
        lax.all_to_all(outgoing_masks, "pair", split_axis=1, concat_axis=1, tiled=True),
    )
    own_row = lax.dynamic_index_in_dim(owners, own_index, 0, keepdims=False)
    own_rank = lax.dynamic_index_in_dim(slot_rank, own_index, 0, keepdims=False)
    slot_index = own_row // block_size * slot_count + own_rank
    received = jnp.take(
        incoming.reshape(window_count, n_pair * slot_count, 2, bin_count), slot_index, axis=1
    )
    received_masks = jnp.take(
        incoming_masks.reshape(incoming_masks.shape[0], n_pair * slot_count), slot_index, axis=1
    ).astype(jnp.float32)
    row_spec = received[:, :PR]
    col_spec = received[:, PR:]
    tallies = jnp.einsum("wc,wr->cr", received_masks[:, PR:], received_masks[:, :PR])
    own_tallies = lax.dynamic_slice_in_dim(tallies, win_index * col_share, col_share, 0)
    stacked = lax.psum_scatter(
        cross_spectra(row_spec, col_spec).astype(jnp.bfloat16),
        "win",
        scatter_dimension=0,
        tiled=True,
    ).astype(jnp.float32)
    row_total = col_share * PR

    def add_block(block_number, running):
        first_bin = block_number * bin_width
        stack_part = lax.dynamic_slice_in_dim(stacked, first_bin, bin_width, 3).reshape(
            row_total, 2 * bin_width
        )
        table = lag_table(first_bin, bin_width, bin_count, lag_count)
        product = jnp.dot(split_three(stack_part), table, preferred_element_type=jnp.float32)
        return (
            running
            + product[:row_total]
            + product[row_total : 2 * row_total]
            + product[2 * row_total :]
        )

    running = lax.fori_loop(
        0, block_count, add_block, jnp.zeros((row_total, lag_count), jnp.float32)
    )
    lagged = running.reshape(col_share, PR, lag_count)
    return lagged / jnp.maximum(own_tallies, 1.0)[:, :, None]


def solution(mesh):
    return jax.shard_map(
        per_device,
        mesh=mesh,
        in_specs=(P("win", "pair", None, None), P("win", "pair"), P()),
        out_specs=P("win", "pair", None),
        check_vma=False,
    )
```

profile of v0, /device:TPU:1, one launch (start us, length us, event | category | flops | bytes accessed | tf_op | source)
XLA Modules:
  0.0 319.0 jit_solution(10997154418018176344)
XLA Ops:
  9.1 2.1 convert_element_type.90
  11.2 5.5 %sqrt_reduce_fusion = f32[32,8192]{1,0:T(8,128)S(1)} fusion(f32[1,32,2,8192]{3,2,1,0:T(2,128)S(1)} %convert_element_type.90), kind=kLoop, calls=%fused_computation.51 | loop fusion | flops 786432 | bytes 3145728 | tf_op jit(solution)/shard_map/sqrt | solution.py:20
  19.0 1.6 broadcast_in_dim.84
  20.6 2.7 fusion.18
  23.4 6.1 %gather_fusion = bf16[64,2,8192]{2,1,0:T(2,128)(2,1)S(1)} fusion(bf16[32,2,8192]{2,1,0:T(2,128)(2,1)S(1)} %fusion.18, s32[1024]{0:T(1024)S(1)} %pad_clamp_fusion.1), kind=kCustom, calls=%fused_computation | custom fusion | bytes 4194560 | tf_op jit(solution)/shard_map/jit(_take)/gather | solution.py:92
  29.5 3.3 %broadcast_select_fusion = bf16[1,32,2,2,8192]{4,3,2,0,1:T(2,128)(2,1)} fusion(bf16[1,32,2,2,8192]{4,3,2,0,1:T(2,128)(2,1)S(1)} %bitcast.96, pred[32,2]{1,0:T(8,128)(4,1)S(1)} %copy.10), kind=kLoop, calls=%fused_computation.43 | loop fusion | flops 1048576 | bytes 4194368 | tf_op jit(solution)/shard_map/jit(_take)/select_n | solution.py:92
  32.8 11.9 %all-to-all-start = ((bf16[1,32,2,2,8192]{4,3,2,0,1:T(2,128)(2,1)}), bf16[1,32,2,2,8192]{4,3,2,0,1:T(2,128)(2,1)S(1)}, u32[]{:S(2)}, u32[]{:S(2)}) async-start(bf16[1,32,2,2,8192]{4,3,2,0,1:T(2,128)(2,1)} %broadcast_select_fusion), calls=%async_computation | async-start | bytes 4194304 | tf_op jit(solution)/shard_map/all_to_all | solution.py:101
  46.4 47.2 %all-to-all-done = bf16[1,32,2,2,8192]{4,3,2,0,1:T(2,128)(2,1)S(1)} async-done(((bf16[1,32,2,2,8192]{4,3,2,0,1:T(2,128)(2,1)}), bf16[1,32,2,2,8192]{4,3,2,0,1:T(2,128)(2,1)S(1)}, u32[]{:S(2)}, u32[]{:S(2)}) %all-to-all-start) | async-done | bytes 2097184 | tf_op jit(solution)/shard_map/all_to_all | solution.py:101
  93.6 2.7 gather_fusion.1
  96.3 1.0 broadcast_select_fusion.1
  97.3 1.7 slice_convert_fusion.3
  100.3 3.5 %fusion.16 = (bf16[16,16,1,8192]{3,1,0,2:T(8,128)(2,1)S(1)}, bf16[16,16,1,8192]{3,1,0,2:T(8,128)(2,1)}) fusion(f32[8192,16]{0,1:T(8,128)S(1)} %bitcast.99, f32[8192,16]{0,1:T(8,128)S(1)} %bitcast.100, f32[8192,16]{0,1:T(8,128)S(1)} %bitcast.101, f32[8192,16]{0,1:T(8,128)S(1)} %bitcast.102), kind=kLoop, calls=%fused_computation.41 | loop fusion | flops 16777216 | bytes 10485760 | tf_op jit(solution)/shard_map/stack | solution.py:56
  103.8 6.2 %pad_maximum_fusion = bf16[16,16,2,8192]{3,1,0,2:T(8,128)(2,1)} fusion(bf16[16,16,1,8192]{3,1,0,2:T(8,128)(2,1)} %get-tuple-element.132, bf16[16,16,1,8192]{3,1,0,2:T(8,128)(2,1)S(1)} %get-tuple-element.131), kind=kLoop, calls=%fused_computation.38 | loop fusion | flops 4194304 | bytes 16777216 | tf_op jit(solution)/shard_map/stack | solution.py:56
  110.0 12.6 %all-gather = s32[8,1,32]{2,1,0:T(1,128)S(1)} all-gather(s32[1,1,32]{2,1,0:T(1,128)S(1)} %bitcast.106), channel_id=1, replica_groups=mesh['win'=8,'pair'=32] {'win'}, dimensions={0}, use_global_device_ids=true | all-gather | bytes 1152 | tf_op jit(solution)/shard_map/all_gather | solution.py:80
  124.0 5.8 %all-to-all-start.1 = ((bf16[8,32,2]{0,2,1:T(2,128)(2,1)}), bf16[8,32,2]{0,2,1:T(2,128)(2,1)S(1)}, u32[]{:S(2)}, u32[]{:S(2)}) async-start(bf16[8,32,2]{0,2,1:T(2,128)(2,1)} %select_convert_fusion), calls=%async_computation.1 | async-start | bytes 32768 | tf_op jit(solution)/shard_map/all_to_all | solution.py:102
  131.2 7.3 %all-to-all-done.1 = bf16[8,32,2]{0,2,1:T(2,128)(2,1)S(1)} async-done(((bf16[8,32,2]{0,2,1:T(2,128)(2,1)}), bf16[8,32,2]{0,2,1:T(2,128)(2,1)S(1)}, u32[]{:S(2)}, u32[]{:S(2)}) %all-to-all-start.1) | async-done | bytes 1056 | tf_op jit(solution)/shard_map/all_to_all | solution.py:102
  139.2 78.8 %all-reduce.3.cloned.1.call-done = bf16[16,16,2,8192]{3,1,0,2:T(8,128)(2,1)} async-done(((bf16[16,16,2,8192]{3,1,0,2:T(8,128)(2,1)}), bf16[16,16,2,8192]{3,1,0,2:T(8,128)(2,1)}) %all-reduce.3.cloned.1.call-update) | async-done | bytes 8388624
  218.1 2.7 dynamic-slice_convert_fusion
  220.8 90.7 %while.16 = (s32[]{:T(128)}, f32[32,512]{1,0:T(8,128)S(1)}, f32[2,16,2,8192]{3,1,0,2:T(8,128)}, s32[]{:T(128)}, s32[]{:T(128)}, /*index=5*/s32[]{:T(128)}, s32[]{:T(128)}) while((s32[]{:T(128)}, f32[32,512]{1,0:T(8,128)S(1)}, f32[2,16,2,8192]{3,1,0,2:T(8,128)}, s32[]{:T(128)}, s32[]{:T(128)}, /*index=5*/s32[]{:T(128)}, ...), condition=%wide.region_5.6_spmd.clone, body=%wide.region_4.5_spmd.clone.sunk | while | flops 216739840 | bytes 7630993 | solution.py:139
  220.8 9.4 %multiply_convert_fusion.4 = (bf16[1024,512]{1,0:T(8,128)(2,1)S(1)}, bf16[1024,512]{1,0:T(8,128)(2,1)S(1)}) fusion(s32[512]{0:T(512)S(1)} %add_select_fusion.6, s32[1024]{0:T(1024)S(1)} %iota_add_fusion.2, f32[1024]{0:T(1024)S(1)} %get-tuple-element.163, f32[1024]{0:T(1024)S(1)} %get-tuple-element.164), kind=kLoop, calls=%fused_computation.17.clone.1 | loop fusion | flops 9437184 | bytes 2111488 | tf_op jit(solution)/shard_map/convert.16
  230.3 1.0 constant_dynamic-slice_fusion.4
  232.2 9.4 %multiply_convert_fusion.4 = (bf16[1024,512]{1,0:T(8,128)(2,1)S(1)}, bf16[1024,512]{1,0:T(8,128)(2,1)S(1)}) fusion(s32[512]{0:T(512)S(1)} %add_select_fusion.6, s32[1024]{0:T(1024)S(1)} %iota_add_fusion.2, f32[1024]{0:T(1024)S(1)} %get-tuple-element.163, f32[1024]{0:T(1024)S(1)} %get-tuple-element.164), kind=kLoop, calls=%fused_computation.17.clone.1 | loop fusion | flops 9437184 | bytes 2111488 | tf_op jit(solution)/shard_map/convert.16
  241.6 1.0 constant_dynamic-slice_fusion.4
  243.5 9.4 %multiply_convert_fusion.4 = (bf16[1024,512]{1,0:T(8,128)(2,1)S(1)}, bf16[1024,512]{1,0:T(8,128)(2,1)S(1)}) fusion(s32[512]{0:T(512)S(1)} %add_select_fusion.6, s32[1024]{0:T(1024)S(1)} %iota_add_fusion.2, f32[1024]{0:T(1024)S(1)} %get-tuple-element.163, f32[1024]{0:T(1024)S(1)} %get-tuple-element.164), kind=kLoop, calls=%fused_computation.17.clone.1 | loop fusion | flops 9437184 | bytes 2111488 | tf_op jit(solution)/shard_map/convert.16
  252.9 1.0 constant_dynamic-slice_fusion.4
  254.8 9.4 %multiply_convert_fusion.4 = (bf16[1024,512]{1,0:T(8,128)(2,1)S(1)}, bf16[1024,512]{1,0:T(8,128)(2,1)S(1)}) fusion(s32[512]{0:T(512)S(1)} %add_select_fusion.6, s32[1024]{0:T(1024)S(1)} %iota_add_fusion.2, f32[1024]{0:T(1024)S(1)} %get-tuple-element.163, f32[1024]{0:T(1024)S(1)} %get-tuple-element.164), kind=kLoop, calls=%fused_computation.17.clone.1 | loop fusion | flops 9437184 | bytes 2111488 | tf_op jit(solution)/shard_map/convert.16
  266.2 9.4 %multiply_convert_fusion.4 = (bf16[1024,512]{1,0:T(8,128)(2,1)S(1)}, bf16[1024,512]{1,0:T(8,128)(2,1)S(1)}) fusion(s32[512]{0:T(512)S(1)} %add_select_fusion.6, s32[1024]{0:T(1024)S(1)} %iota_add_fusion.2, f32[1024]{0:T(1024)S(1)} %get-tuple-element.163, f32[1024]{0:T(1024)S(1)} %get-tuple-element.164), kind=kLoop, calls=%fused_computation.17.clone.1 | loop fusion | flops 9437184 | bytes 2111488 | tf_op jit(solution)/shard_map/convert.16
  277.5 9.4 %multiply_convert_fusion.4 = (bf16[1024,512]{1,0:T(8,128)(2,1)S(1)}, bf16[1024,512]{1,0:T(8,128)(2,1)S(1)}) fusion(s32[512]{0:T(512)S(1)} %add_select_fusion.6, s32[1024]{0:T(1024)S(1)} %iota_add_fusion.2, f32[1024]{0:T(1024)S(1)} %get-tuple-element.163, f32[1024]{0:T(1024)S(1)} %get-tuple-element.164), kind=kLoop, calls=%fused_computation.17.clone.1 | loop fusion | flops 9437184 | bytes 2111488 | tf_op jit(solution)/shard_map/convert.16
  286.9 1.0 constant_dynamic-slice_fusion.4
  288.9 9.4 %multiply_convert_fusion.4 = (bf16[1024,512]{1,0:T(8,128)(2,1)S(1)}, bf16[1024,512]{1,0:T(8,128)(2,1)S(1)}) fusion(s32[512]{0:T(512)S(1)} %add_select_fusion.6, s32[1024]{0:T(1024)S(1)} %iota_add_fusion.2, f32[1024]{0:T(1024)S(1)} %get-tuple-element.163, f32[1024]{0:T(1024)S(1)} %get-tuple-element.164), kind=kLoop, calls=%fused_computation.17.clone.1 | loop fusion | flops 9437184 | bytes 2111488 | tf_op jit(solution)/shard_map/convert.16
  298.3 1.0 constant_dynamic-slice_fusion.4
  300.2 9.4 %multiply_convert_fusion.4 = (bf16[1024,512]{1,0:T(8,128)(2,1)S(1)}, bf16[1024,512]{1,0:T(8,128)(2,1)S(1)}) fusion(s32[512]{0:T(512)S(1)} %add_select_fusion.6, s32[1024]{0:T(1024)S(1)} %iota_add_fusion.2, f32[1024]{0:T(1024)S(1)} %get-tuple-element.163, f32[1024]{0:T(1024)S(1)} %get-tuple-element.164), kind=kLoop, calls=%fused_computation.17.clone.1 | loop fusion | flops 9437184 | bytes 2111488 | tf_op jit(solution)/shard_map/convert.16
  (113 shorter events, 21.1 us)
Async XLA Ops:
  16.8 0.9 copy-start
  32.8 60.8 %all-to-all-start = ((bf16[1,32,2,2,8192]{4,3,2,0,1:T(2,128)(2,1)}), bf16[1,32,2,2,8192]{4,3,2,0,1:T(2,128)(2,1)S(1)}, u32[]{:S(2)}, u32[]{:S(2)}) async-start(bf16[1,32,2,2,8192]{4,3,2,0,1:T(2,128)(2,1)} %broadcast_select_fusion), calls=%async_computation | async-start | bytes 4194304 | tf_op jit(solution)/shard_map/all_to_all | solution.py:101
  44.7 173.4 %all-reduce.3.cloned.1.call-start = ((), (), s32[]{:S(2)}) async-start(), calls=%async_computation.2 | async-start | bytes 16777216
  110.0 19.9 %copy-start.1 = (u32[256]{0:T(256)S(1)}, u32[256]{0:T(256)}, u32[]{:S(2)}) copy-start(u32[256]{0:T(256)} %constant.245) | copy-start | bytes 3076
  124.0 14.4 %all-to-all-start.1 = ((bf16[8,32,2]{0,2,1:T(2,128)(2,1)}), bf16[8,32,2]{0,2,1:T(2,128)(2,1)S(1)}, u32[]{:S(2)}, u32[]{:S(2)}) async-start(bf16[8,32,2]{0,2,1:T(2,128)(2,1)} %select_convert_fusion), calls=%async_computation.1 | async-start | bytes 32768 | tf_op jit(solution)/shard_map/all_to_all | solution.py:102
Sparse Core Ops, SparseCore 0:
  110.1 107.9 all-reduce.2
where the time goes:
time: 320 us; the launch traced here: 319 us
  waiting for transfers between devices  133 us (42%)
  other arithmetic  111 us (35%)
  local copies, waits for them, and re-layouts  25.4 us (8%)
  starting transfers between devices  17.9 us (6%)
  between operations  14.3 us (4%)
  blocking collectives  12.6 us (4%)
  matrix products  3.82 us (1%)
    unnamed x2, waiting for transfers between devices  78.9 us
    another operation x9, other arithmetic  76.9 us
    all_to_all x1, waiting for transfers between devices, per_device(): lax.all_to_all(outgoing, 'pair', split_axis=1, concat_axis=1, tiled=True)  47.2 us
    all_gather x1, blocking collectives, per_device(): mask_table = lax.all_gather(availability, 'win', axis=0, tiled=True)  12.6 us
    all_to_all x1, starting transfers between devices, per_device(): lax.all_to_all(outgoing, 'pair', split_axis=1, concat_axis=1, tiled=True)  11.9 us
    another operation x2, other arithmetic, cross_spectra(): return jnp.stack([real_part, imag_part], axis=2)  9.7 us
    dynamic_slice x16, local copies, waits for them, and re-layouts, add_block(): lax.dynamic_slice_in_dim(stacked, first_bin, bin_width, 3)  9.43 us
    all_to_all x1, waiting for transfers between devices, per_device(): lax.all_to_all(outgoing_masks, 'pair', split_axis=1, concat_axis=1, tiled...  7.27 us
  transfers between devices with their start and end apart: 3, of which 3 were waited for; matrix products, arithmetic and copies ran while one was open for 1% of the time, Pallas kernels for 0%

commit v1 on v0

v1 whole, which is shorter than its diff:
```python
import functools
import math

import jax
import jax.numpy as jnp
from jax import lax
from jax.experimental import pallas as pl
from jax.experimental.pallas import tpu as pltpu
from jax.sharding import PartitionSpec as P

WB = 64
LAGS = 512
PR = 16
PC = 16
NEED = 32
EPSILON = 1e-06

NX, NZ = 4, 8
N_PAIR = NX * NZ
N_WIN = 8
BLOCK = 32
BINS = 8192
CHUNK = BINS // N_WIN
SUBS = 4
SUB = CHUNK // SUBS
MSG = 16
ROWS = N_PAIR * MSG
PERIOD = 2 * BINS
FINE = 32

f32 = jnp.float32
bf16 = jnp.bfloat16
i32 = jnp.int32

OFFSETS = [
    (dx, dz) for dz in (4, 3, -3, 2, -2, 1, -1, 0) for dx in (2, 1, -1, 0) if (dx, dz) != (0, 0)
]


def iota(shape, dim):
    return lax.broadcasted_iota(i32, shape, dim)


def kernel(
    x_ref,
    own_ref,
    avail_ref,
    out_ref,
    recv1,
    send2,
    recv2,
    table,
    lhs,
    acc,
    smat,
    rmat,
    cos_a,
    sin_a,
    mask_send,
    mask_recv,
    tal_send,
    tal_recv,
    lag_send,
    lag_recv,
    s1_send,
    s1_recv,
    s2_send,
    s2_recv,
    m_send,
    m_recv,
    t_send,
    t_recv,
    l_send,
    l_recv,
):
    me_w = lax.axis_index("win")
    me_p = lax.axis_index("pair")
    x, z = me_p // NZ, me_p % NZ
    pair_peers = [((x + dx + NX) % NX) * NZ + (z + dz + NZ) % NZ for dx, dz in OFFSETS]

    def win_peer(t):
        return (me_w + t) % N_WIN

    barrier = pltpu.get_barrier_semaphore()
    for q in pair_peers:
        pl.semaphore_signal(barrier, inc=1, device_id={"pair": q})
    for t in range(1, N_WIN):
        pl.semaphore_signal(barrier, inc=1, device_id={"win": win_peer(t)})

    owners = own_ref[...]
    spread = (iota((ROWS, N_PAIR), 0) // MSG == iota((ROWS, N_PAIR), 1)).astype(bf16)
    block = jnp.dot(spread, (owners // BLOCK).astype(bf16), preferred_element_type=f32).astype(i32)
    station = jnp.dot(spread, (owners % BLOCK).astype(bf16), preferred_element_type=f32).astype(i32)
    mine = block == me_p
    first = jnp.min(jnp.where(mine, station, BLOCK - 1), axis=1, keepdims=True)
    last = jnp.max(jnp.where(mine, station, 0), axis=1, keepdims=True)
    row = iota((ROWS, 1), 0) % MSG
    wanted = jnp.where((row % 4) // 2 == 0, first, last)
    source = (row // 4) * (2 * BLOCK) + 2 * wanted + row % 2
    smat[...] = (iota((ROWS, SUBS * 2 * BLOCK), 1) == source).astype(bf16)
    mask_row = avail_ref[...].astype(f32)
    mask_send[...] = jnp.concatenate([mask_row, jnp.zeros((1, 128 - BLOCK), f32)], axis=1)
    mask_recv[me_p] = mask_send[...]

    pl.semaphore_wait(barrier, len(pair_peers) + N_WIN - 1)

    def phase1(t):
        chunk = pl.ds(pl.multiple_of(win_peer(t) * CHUNK, CHUNK), CHUNK)
        return pltpu.make_async_remote_copy(
            src_ref=x_ref.at[:, chunk],
            dst_ref=recv1.at[t],
            send_sem=s1_send.at[t],
            recv_sem=s1_recv.at[t],
            device_id={"win": win_peer(t)},
        )

    for t in range(1, N_WIN):
        phase1(t).start()

    def send_window(t, block_value):
        stacked = jnp.concatenate(
            [block_value[:, SUB * s : SUB * (s + 1)] for s in range(SUBS)], axis=0
        )
        message = jnp.dot(smat[...], stacked, preferred_element_type=f32).astype(bf16)
        send2[t] = message
        here = pl.ds(pl.multiple_of(me_p * MSG, MSG), MSG)
        for q in pair_peers:
            there = pl.ds(pl.multiple_of(q * MSG, MSG), MSG)
            pltpu.make_async_remote_copy(
                src_ref=send2.at[t, there],
                dst_ref=recv2.at[t, here],
                send_sem=s2_send.at[t],
                recv_sem=s2_recv.at[t],
                device_id={"pair": q},
            ).start()
        recv2[t, here, :] = send2[t, here, :]

    own_chunk = pl.ds(pl.multiple_of(me_w * CHUNK, CHUNK), CHUNK)
    send_window(0, x_ref[:, own_chunk])
    for q in pair_peers:
        pltpu.make_async_remote_copy(
            src_ref=mask_send,
            dst_ref=mask_recv.at[me_p],
            send_sem=m_send,
            recv_sem=m_recv,
            device_id={"pair": q},
        ).start()

    own_row = own_ref[pl.ds(me_p, 1), :]

    def pick(rows, lane):
        hit = iota((rows, NEED), 1) == lane
        return jnp.sum(jnp.where(hit, own_row, 0), axis=1, keepdims=True)

    sel_rows = SUBS * 2 * NEED
    sel = iota((sel_rows, 1), 0)
    chosen = pick(sel_rows, sel % NEED)
    earlier = jnp.logical_and(own_row // BLOCK == chosen // BLOCK, own_row < chosen)
    slot = jnp.max(earlier.astype(i32), axis=1, keepdims=True)
    target = (
        (chosen // BLOCK) * MSG + (sel // (2 * NEED)) * 4 + slot * 2 + (sel // NEED) % 2
    )
    rmat[...] = (iota((sel_rows, ROWS), 1) == target).astype(bf16)
    band = jnp.where(
        iota((SUB, SUB), 0) // WB == iota((SUB, SUB), 1) // WB, 1.0 / WB, 0.0
    ).astype(bf16)

    lag = iota((FINE, LAGS), 1) - LAGS // 2
    index = iota((FINE, LAGS), 0)

    def angle(phase):
        phase = jnp.bitwise_and(phase + PERIOD // 2, PERIOD - 1) - PERIOD // 2
        return phase.astype(f32) * (2.0 * math.pi / PERIOD)

    coarse = angle((me_w * CHUNK + FINE * index) * lag)
    cos_a[...] = jnp.cos(coarse)
    sin_a[...] = jnp.sin(coarse)
    fine = angle(index * lag)
    cos_b, sin_b = jnp.cos(fine), jnp.sin(fine)

    def table_rows(n, carry):
        ca, sa = cos_a[pl.ds(n, 1), :], sin_a[pl.ds(n, 1), :]
        bins = me_w * CHUNK + FINE * n + iota((FINE, 1), 0)
        weight = jnp.where(bins == 0, 1.0, 2.0) / math.sqrt(PERIOD)
        at = pl.multiple_of(n * FINE, FINE)
        table[pl.ds(at, FINE), :] = (weight * (ca * cos_b - sa * sin_b)).astype(bf16)
        table[pl.ds(CHUNK + at, FINE), :] = (-weight * (sa * cos_b + ca * sin_b)).astype(bf16)
        return carry

    lax.fori_loop(0, CHUNK // FINE, table_rows, 0)

    def relay(t, carry):
        phase1(t).wait_recv()
        send_window(t, recv1[t])
        return carry

    lax.fori_loop(1, N_WIN, relay, 0)

    pltpu.make_async_copy(
        mask_recv.at[pl.ds(0, N_PAIR - 1)], mask_recv.at[pl.ds(0, N_PAIR - 1)], m_recv
    ).wait()
    masks = mask_recv[:, 0, :].astype(bf16)
    pairs = PC * PR
    pair = iota((pairs, 1), 0)

    def mask_of(lane):
        who = pick(pairs, lane)
        where = (iota((pairs, N_PAIR), 1) == who // BLOCK).astype(bf16)
        lines = jnp.dot(where, masks, preferred_element_type=f32)
        hit = iota((pairs, 128), 1) == who % BLOCK
        return jnp.sum(jnp.where(hit, lines, 0.0), axis=1, keepdims=True)

    both = mask_of(pair % PR) * mask_of(PR + pair // PR)
    tal_send[...] = jnp.broadcast_to(both, (pairs, 128)).astype(bf16)
    share = pairs // N_WIN

    def tally(t):
        rows = pl.ds(pl.multiple_of(win_peer(t) * share, share), share)
        return pltpu.make_async_remote_copy(
            src_ref=tal_send.at[rows],
            dst_ref=tal_recv.at[t],
            send_sem=t_send.at[t],
            recv_sem=t_recv.at[t],
            device_id={"win": win_peer(t)},
        )

    for t in range(1, N_WIN):
        tally(t).start()

    acc[...] = jnp.zeros_like(acc)

    def window(t, carry):
        others = recv2.at[t, pl.ds(0, ROWS - MSG)]
        pltpu.make_async_copy(others, others, s2_recv.at[t]).wait()
        chosen_rows = jnp.dot(rmat[...], recv2[t], preferred_element_type=f32)
        for s in range(SUBS):
            re = chosen_rows[2 * NEED * s : 2 * NEED * s + NEED]
            im = chosen_rows[2 * NEED * s + NEED : 2 * NEED * (s + 1)]
            magnitude = jnp.sqrt(re * re + im * im)
            upper = magnitude.astype(bf16)
            lower = (magnitude - upper.astype(f32)).astype(bf16)
            level = jnp.dot(upper, band, preferred_element_type=f32) + jnp.dot(
                lower, band, preferred_element_type=f32
            )
            factor = 1.0 / (level + EPSILON)
            white_re = (re * factor).astype(bf16).astype(f32)
            white_im = (im * factor).astype(bf16).astype(f32)
            ar, ai = white_re[:PR], white_im[:PR]
            for j in range(PC):
                br, bi = white_re[PR + j : PR + j + 1], white_im[PR + j : PR + j + 1]
                rows = slice(PR * j, PR * (j + 1))
                lhs[rows, SUB * s : SUB * (s + 1)] = (ar * br + ai * bi).astype(bf16)
                lhs[rows, CHUNK + SUB * s : CHUNK + SUB * (s + 1)] = (ai * br - ar * bi).astype(
                    bf16
                )
        acc[...] += jnp.dot(lhs[...], table[...], preferred_element_type=f32)
        return carry

    lax.fori_loop(0, N_WIN, window, 0)

    lag_send[...] = acc[...].astype(bf16)

    def lagged(t):
        rows = pl.ds(pl.multiple_of(win_peer(t) * share, share), share)
        return pltpu.make_async_remote_copy(
            src_ref=lag_send.at[rows],
            dst_ref=lag_recv.at[t],
            send_sem=l_send.at[t],
            recv_sem=l_recv.at[t],
            device_id={"win": win_peer(t)},
        )

    for t in range(1, N_WIN):
        lagged(t).start()
    own = pl.ds(pl.multiple_of(me_w * share, share), share)
    count = tal_send[own, :].astype(f32)
    for t in range(1, N_WIN):
        tally(t).wait_recv()
        count = count + tal_recv[t].astype(f32)
    total = acc[own, :]
    for t in range(1, N_WIN):
        lagged(t).wait_recv()
        total = total + lag_recv[t].astype(f32)
    out_ref[...] = total / jnp.maximum(count[:, :1], 1.0)

    for t in range(1, N_WIN):
        phase1(t).wait_send()
        tally(t).wait_send()
        lagged(t).wait_send()
    pltpu.make_async_copy(
        mask_recv.at[pl.ds(0, N_PAIR - 1)], mask_recv.at[pl.ds(0, N_PAIR - 1)], m_send
    ).wait()
    for t in range(N_WIN):
        others = send2.at[t, pl.ds(0, ROWS - MSG)]
        pltpu.make_async_copy(others, others, s2_send.at[t]).wait()


def per_device(spectra, availability, owners):
    masked = spectra[0] * availability[0].astype(bf16)[:, None, None]
    masked = masked.reshape(2 * BLOCK, BINS)
    pairs = PC * PR
    share = pairs // N_WIN
    dma = pltpu.SemaphoreType.DMA
    vmem = pl.BlockSpec(memory_space=pltpu.VMEM)
    out = pl.pallas_call(
        kernel,
        out_shape=jax.ShapeDtypeStruct((share, LAGS), f32),
        in_specs=[vmem] * 3,
        out_specs=vmem,
        scratch_shapes=[
            pltpu.VMEM((N_WIN, 2 * BLOCK, CHUNK), bf16),
            pltpu.VMEM((N_WIN, ROWS, SUB), bf16),
            pltpu.VMEM((N_WIN, ROWS, SUB), bf16),
            pltpu.VMEM((2 * CHUNK, LAGS), bf16),
            pltpu.VMEM((pairs, 2 * CHUNK), bf16),
            pltpu.VMEM((pairs, LAGS), f32),
            pltpu.VMEM((ROWS, SUBS * 2 * BLOCK), bf16),
            pltpu.VMEM((SUBS * 2 * NEED, ROWS), bf16),
            pltpu.VMEM((CHUNK // FINE, LAGS), f32),
            pltpu.VMEM((CHUNK // FINE, LAGS), f32),
            pltpu.VMEM((1, 128), f32),
            pltpu.VMEM((N_PAIR, 1, 128), f32),
            pltpu.VMEM((pairs, 128), bf16),
            pltpu.VMEM((N_WIN, share, 128), bf16),
            pltpu.VMEM((pairs, LAGS), bf16),
            pltpu.VMEM((N_WIN, share, LAGS), bf16),
            dma((N_WIN,)),
            dma((N_WIN,)),
            dma((N_WIN,)),
            dma((N_WIN,)),
            dma,
            dma,
            dma((N_WIN,)),
            dma((N_WIN,)),
            dma((N_WIN,)),
            dma((N_WIN,)),
        ],
        compiler_params=pltpu.CompilerParams(
            collective_id=0, has_side_effects=True, vmem_limit_bytes=48 * 1024 * 1024
        ),
        cost_estimate=pl.CostEstimate(
            flops=6_000_000_000, bytes_accessed=2_000_000, transcendentals=1_000_000
        ),
    )(masked, owners, availability)
    return out.reshape(PC // N_WIN, PR, LAGS)


def solution(mesh):
    return jax.shard_map(
        per_device,
        mesh=mesh,
        in_specs=(P("win", "pair", None, None), P("win", "pair"), P()),
        out_specs=P("win", "pair", None),
        check_vma=False,
    )
```

time: 320 us -> 69.9 us (0.22)
  waiting for transfers between devices: 133 us -> 0 us
  other arithmetic: 111 us -> 0.8 us
  Pallas kernels: 0 us -> 66 us
  local copies, waits for them, and re-layouts: 25.4 us -> 2.85 us
  starting transfers between devices: 17.9 us -> 0 us
  between operations: 14.3 us -> 0.04 us
  blocking collectives: 12.6 us -> 0 us
  matrix products: 3.82 us -> 0 us
    another operation x11 -> x0, other arithmetic: 86.6 us -> none
    unnamed x2 -> x0, waiting for transfers between devices: 78.9 us -> none
    pallas_call x0 -> x1, Pallas kernels: none -> 66 us  [per_device(): pl.pallas_call(kernel, out_shape=jax.ShapeDtypeStruct((share, LAGS), f32)...]
    all_to_all x2 -> x0, waiting for transfers between devices: 54.5 us -> none  [the longest x1 47.2 us: per_device(): lax.all_to_all(outgoing, 'pair', split_axis=1, concat_axis=1, tiled=True)]
    all_to_all x2 -> x0, starting transfers between devices: 17.7 us -> none  [the longest x1 11.9 us: per_device(): lax.all_to_all(outgoing, 'pair', split_axis=1, concat_axis=1, tiled=True)]
    all_gather x1 -> x0, blocking collectives: 12.6 us -> none  [per_device(): mask_table = lax.all_gather(availability, 'win', axis=0, tiled=True)]
    gather x4 -> x0, local copies, waits for them, and re-layouts: 9.95 us -> none  [the longest x1 6.11 us: per_device(): jnp.take(whitened, local_station, axis=1)]
    dynamic_slice x16 -> x0, local copies, waits for them, and re-layouts: 9.43 us -> none  [add_block(): lax.dynamic_slice_in_dim(stacked, first_bin, bin_width, 3)]
  transfers between devices with their start and end apart: 3 -> 0, of which waited for: 3 -> 0; matrix products, arithmetic and copies ran while one was open for 1% -> 0% of each run, Pallas kernels for 0% -> 0%
where the time goes in v1:
time: 69.9 us; the launch traced here: 69.7 us
  Pallas kernels  66 us (94%)
  local copies, waits for them, and re-layouts  2.85 us (4%)
  other arithmetic  0.8 us (1%)
    pallas_call x1, Pallas kernels, per_device(): pl.pallas_call(kernel, out_shape=jax.ShapeDtypeStruct((share, LAGS), f32)...  66 us
    squeeze x1, local copies, waits for them, and re-layouts, per_device(): masked = spectra[0] * availability[0].astype(bf16)[:, None, None]  1.47 us

profile of v1, /device:TPU:1, one launch (start us, length us, event | category | flops | bytes accessed | tf_op | source)
XLA Modules:
  0.0 69.7 jit_solution(2840727598818997963)
XLA Ops:
  0.0 0.7 convert_bitcast_fusion
  0.7 0.1 mul.13
  0.7 0.1 mul.14
  0.8 1.5 %squeeze.4 = bf16[64,8192]{1,0:T(8,128)(2,1)S(1)} reshape(bf16[1,32,2,8192]{3,2,1,0:T(2,128)(2,1)} %param.3) | data formatting | bytes 2097152 | tf_op jit(solution)/shard_map/squeeze | solution.py:299
  2.3 0.0 copy-start
  2.3 0.0 copy-start.1
  2.3 0.1 broadcast_multiply_fusion.x_ref
  2.5 0.6 copy-done
  3.0 0.0 copy-done.1
  3.0 66.0 %shard_map.37 = f32[32,512]{1,0:T(8,128)S(1)} custom-call(bf16[64,8192]{1,0:T(8,128)(2,1)S(1)} %broadcast_multiply_fusion.x_ref, s32[32,32]{1,0:T(8,128)S(1)} %copy-done, s32[1,32]{1,0:T(1,128)S(1)} %copy-done.1), custom_call_target="tpu_custom_call" | custom-call | flops 6000000000 | bytes 2000000 | tf_op jit(solution)/shard_map/pallas_call | solution.py:305
  69.1 0.6 copy.5
Async XLA Ops:
  2.3 0.7 %copy-start = (s32[32,32]{1,0:T(8,128)S(1)}, s32[32,32]{1,0:T(8,128)}, u32[]{:S(2)}) copy-start(s32[32,32]{1,0:T(8,128)} %own_ref.1) | copy-start | bytes 12292
  2.3 0.7 %copy-start.1 = (s32[1,32]{1,0:T(1,128)S(1)}, s32[1,32]{1,0:T(1,128)}, u32[]{:S(2)}) copy-start(s32[1,32]{1,0:T(1,128)} %avail_ref.1) | copy-start | bytes 388

commit v2 on v0

v2 whole, which is shorter than its diff:
```python
import math

import jax
import jax.numpy as jnp
from jax import lax
from jax.experimental import pallas as pl
from jax.experimental.pallas import tpu as pltpu
from jax.sharding import PartitionSpec as P

WB = 64
LAGS = 512
PR = 16
PC = 16
NEED = 32
EPSILON = 1e-06

NX, NZ = 4, 8
N_PAIR = NX * NZ
N_WIN = 8
BLOCK = 32
BINS = 8192
CHUNK = BINS // NZ
STEPS = 4
SUB = CHUNK // STEPS
AHEAD = 2
PLANE = NX * N_WIN
HALVES = 2
QUAD = NZ // HALVES
MSG = 4 * NZ
PERIOD = 2 * BINS
FINE = 32
PAIRS = PC * PR
SHARE = PAIRS // N_WIN

f32 = jnp.float32
bf16 = jnp.bfloat16
i32 = jnp.int32

Z_OFFSETS = [4, 3, -3, 2, -2, 1, -1]
PLANE_OFFSETS = [(dw, dx) for dw in (4, 3, 5, 2, 6, 1, 7, 0) for dx in (2, 1, -1, 0)][:-1]


def iota(shape, dim):
    return lax.broadcasted_iota(i32, shape, dim)


def kernel(
    x_hbm,
    own_hbm,
    avail_hbm,
    out_ref,
    x_ref,
    own_ref,
    avail_ref,
    recv1,
    send2,
    recv2,
    table,
    white,
    lhs,
    acc,
    smat,
    cos_a,
    sin_a,
    mask_z,
    mask_all,
    present,
    final_present,
    lag_send,
    lag_held,
    lag_recv,
    in_sem,
    d_send,
    d_recv,
    s_send,
    s_recv,
    m_send,
    m_recv,
    l_send,
    l_recv,
    f_send,
    f_recv,
):
    me_w = lax.axis_index("win")
    me_p = lax.axis_index("pair")
    x, z = me_p // NZ, me_p % NZ
    z_peers = [(z + dz + NZ) % NZ for dz in Z_OFFSETS]
    plane_peers = [((me_w + dw) % N_WIN, (x + dx + NX) % NX) for dw, dx in PLANE_OFFSETS]

    barrier = pltpu.get_barrier_semaphore()
    for k in z_peers:
        pl.semaphore_signal(barrier, inc=1, device_id={"pair": x * NZ + k})
    for o, k in plane_peers:
        pl.semaphore_signal(barrier, inc=1, device_id={"win": o, "pair": k * NZ + z})
    own_in = pltpu.make_async_copy(own_hbm, own_ref, in_sem.at[0])
    avail_in = pltpu.make_async_copy(avail_hbm, avail_ref, in_sem.at[1])
    x_in = pltpu.make_async_copy(x_hbm.at[0], x_ref, in_sem.at[2])
    own_in.start()
    avail_in.start()
    x_in.start()
    avail_in.wait()
    mask_z[z] = jnp.concatenate(
        [avail_ref[...].astype(f32), jnp.zeros((1, 128 - BLOCK), f32)], axis=1
    )
    x_in.wait()
    pl.semaphore_wait(barrier, NZ - 1 + PLANE - 1)


    def spectra_step(s, k):
        bins = pl.ds(pl.multiple_of(k * CHUNK + s * SUB, SUB), SUB)
        return x_ref.at[:, :, bins]

    def start_spectra(s):
        for k in z_peers:
            pltpu.make_async_remote_copy(
                src_ref=spectra_step(s, k),
                dst_ref=recv1.at[s, z],
                send_sem=d_send.at[s],
                recv_sem=d_recv.at[s],
                device_id={"pair": x * NZ + k},
            ).start()
        pltpu.make_async_copy(spectra_step(s, z), recv1.at[s, z], d_recv.at[s]).start()

    for k in z_peers:
        pltpu.make_async_remote_copy(
            src_ref=mask_z.at[z],
            dst_ref=mask_z.at[z],
            send_sem=m_send.at[0],
            recv_sem=m_recv.at[0],
            device_id={"pair": x * NZ + k},
        ).start()

    for s in range(AHEAD):
        start_spectra(s)
    own_in.wait()

    rows = 16 * N_PAIR
    owners = own_ref[...]
    spread = (iota((rows, N_PAIR), 0) >> 4 == iota((rows, N_PAIR), 1)).astype(bf16)
    block = jnp.dot(spread, (owners >> 5).astype(bf16), preferred_element_type=f32)
    station = jnp.dot(spread, (owners & 31).astype(bf16), preferred_element_type=f32)
    row = iota((rows, 1), 0)
    near = (row >> 2) & 3
    upper_slot = ((row >> 1) & 1) == 1
    for half in range(HALVES):
        mine = block == (x * NZ + half * QUAD + near).astype(f32)
        first = jnp.min(jnp.where(mine, station, BLOCK - 1.0), axis=1, keepdims=True)
        last = jnp.max(jnp.where(mine, station, 0.0), axis=1, keepdims=True)
        wanted = jnp.where(upper_slot, last, first).astype(i32)
        source = near * (2 * BLOCK) + 2 * wanted + (row & 1)
        smat[half] = (iota((rows, QUAD * 2 * BLOCK), 1) == source).astype(bf16)

    near_masks = mask_z.at[pl.ds(0, NZ - 1)]
    pltpu.make_async_copy(near_masks, near_masks, m_recv.at[0]).wait()
    here = pl.ds((me_w * NX + x) * NZ, NZ)
    for o, k in plane_peers:
        pltpu.make_async_remote_copy(
            src_ref=mask_z,
            dst_ref=mask_all.at[here],
            send_sem=m_send.at[1],
            recv_sem=m_recv.at[1],
            device_id={"win": o, "pair": k * NZ + z},
        ).start()
    mask_all[here] = mask_z[...]
    far_masks = mask_all.at[pl.ds(0, N_WIN * N_PAIR - NZ)]

    def relay(s):
        whole = recv1.at[s]
        pltpu.make_async_copy(whole, whole, d_recv.at[s]).wait()

        @pl.when(s + AHEAD < STEPS)
        def _():
            start_spectra(s + AHEAD)

        for half in range(HALVES):
            stations = recv1[s, half * QUAD : (half + 1) * QUAD].reshape(QUAD * 2 * BLOCK, SUB)
            message = jnp.dot(smat[half], stations, preferred_element_type=f32).astype(bf16)
            send2[s, :, 16 * half : 16 * (half + 1), :] = message.reshape(N_PAIR, 16, SUB)
        for o, k in plane_peers:
            pltpu.make_async_remote_copy(
                src_ref=send2.at[s, k * NZ + o],
                dst_ref=recv2.at[s, me_w * NX + x],
                send_sem=s_send.at[s],
                recv_sem=s_recv.at[s],
                device_id={"win": o, "pair": k * NZ + z},
            ).start()
        recv2[s, me_w * NX + x] = send2[s, x * NZ + me_w]

    def process(s):
        others = recv2.at[s, pl.ds(0, PLANE - 1)]
        pltpu.make_async_copy(others, others, s_recv.at[s]).wait()
        for w in range(N_WIN):
            messages = recv2[s, NX * w : NX * (w + 1)].reshape(NX * MSG, SUB)
            lines = jnp.dot(rmat, messages, preferred_element_type=f32)
            re, im = lines[:NEED], lines[NEED:]
            magnitude = jnp.sqrt(re * re + im * im)
            upper = magnitude.astype(bf16)
            lower = (magnitude - upper.astype(f32)).astype(bf16)
            level = jnp.dot(upper, band, preferred_element_type=f32) + jnp.dot(
                lower, band, preferred_element_type=f32
            )
            factor = present[NEED * w : NEED * (w + 1), :1] / (level + EPSILON)
            white[w, 0] = (re * factor).astype(bf16).astype(f32)
            white[w, 1] = (im * factor).astype(bf16).astype(f32)
        for j in range(PC):
            total_re = jnp.zeros((PR, SUB), f32)
            total_im = jnp.zeros((PR, SUB), f32)
            for w in range(N_WIN):
                ar, ai = white[w, 0, :PR, :], white[w, 1, :PR, :]
                br = white[w, 0, PR + j : PR + j + 1, :]
                bi = white[w, 1, PR + j : PR + j + 1, :]
                total_re = total_re + (ar * br + ai * bi)
                total_im = total_im + (ai * br - ar * bi)
            for part, total in enumerate((total_re, total_im)):
                upper = total.astype(bf16)
                lower = (total - upper.astype(f32)).astype(bf16)
                lhs[PR * j : PR * (j + 1), SUB * part : SUB * (part + 1)] = upper
                lhs[PAIRS + PR * j : PAIRS + PR * (j + 1), SUB * part : SUB * (part + 1)] = lower
        product = jnp.dot(lhs[...], table[s], preferred_element_type=f32)
        acc[...] += product[:PAIRS] + product[PAIRS:]

    relay(0)

    lag = iota((FINE, LAGS), 1) - LAGS // 2
    index = iota((FINE, LAGS), 0)

    def angle(phase):
        phase = ((phase + PERIOD // 2) & (PERIOD - 1)) - PERIOD // 2
        return phase.astype(f32) * (2.0 * math.pi / PERIOD)

    coarse = angle((z * CHUNK + FINE * index) * lag)
    cos_a[...] = jnp.cos(coarse)
    sin_a[...] = jnp.sin(coarse)
    fine = angle(index * lag)
    cos_b, sin_b = jnp.cos(fine), jnp.sin(fine)

    def table_rows(n, carry):
        ca, sa = cos_a[pl.ds(n, 1), :], sin_a[pl.ds(n, 1), :]
        bins = z * CHUNK + FINE * n + iota((FINE, 1), 0)
        weight = jnp.where(bins == 0, 1.0, 2.0) / math.sqrt(PERIOD)
        s = n // (SUB // FINE)
        at = pl.multiple_of(n % (SUB // FINE) * FINE, FINE)
        table[s, pl.ds(at, FINE), :] = (weight * (ca * cos_b - sa * sin_b)).astype(bf16)
        table[s, pl.ds(SUB + at, FINE), :] = (-weight * (sa * cos_b + ca * sin_b)).astype(bf16)
        return carry

    lax.fori_loop(0, CHUNK // FINE, table_rows, 0)

    def pick(count, lane, own_row):
        hit = iota((count, NEED), 1) == lane
        return jnp.sum(jnp.where(hit, own_row, 0), axis=1, keepdims=True)

    work_row = own_ref[pl.ds(x * NZ + me_w, 1), :]
    sel = iota((2 * NEED, 1), 0)
    chosen = pick(2 * NEED, sel & (NEED - 1), work_row)
    earlier = jnp.logical_and(work_row >> 5 == chosen >> 5, work_row < chosen)
    slot = jnp.max(earlier.astype(f32), axis=1, keepdims=True).astype(i32)
    target = (chosen >> 5) * 4 + slot * 2 + (sel >> 5)
    rmat = (iota((2 * NEED, NX * MSG), 1) == target).astype(bf16)
    band = jnp.where(iota((SUB, SUB), 0) >> 6 == iota((SUB, SUB), 1) >> 6, 1.0 / WB, 0.0)
    band = band.astype(bf16)
    acc[...] = jnp.zeros_like(acc)

    line = iota((N_WIN * NEED, 1), 0)

    def availability_of(masks, own_row):
        who = pick(N_WIN * NEED, line & (NEED - 1), own_row)
        place = (line >> 5) * N_PAIR + (who >> 5)
        where = (iota((N_WIN * NEED, N_WIN * N_PAIR), 1) == place).astype(bf16)
        found = jnp.dot(where, masks, preferred_element_type=f32)
        hit = iota((N_WIN * NEED, 128), 1) == who & 31
        value = jnp.sum(jnp.where(hit, found, 0.0), axis=1, keepdims=True)
        return jnp.broadcast_to(value, (N_WIN * NEED, 128))


    def step(s, carry):
        @pl.when(s < STEPS)
        def _():
            relay(s)

        @pl.when(s == 1)
        def _():
            pltpu.make_async_copy(far_masks, far_masks, m_recv.at[1]).wait()
            masks = mask_all[:, 0, :].astype(bf16)
            present[...] = availability_of(masks, work_row)
            final_present[...] = availability_of(masks, own_ref[pl.ds(me_p, 1), :])

        process(s - 1)
        return carry

    lax.fori_loop(1, STEPS + 1, step, 0)

    lag_send[...] = acc[...].astype(bf16).reshape(N_WIN, SHARE, LAGS)

    def across(t):
        o = (me_w + t) % N_WIN
        return pltpu.make_async_remote_copy(
            src_ref=lag_send.at[o],
            dst_ref=lag_held.at[t],
            send_sem=l_send.at[t],
            recv_sem=l_recv.at[t],
            device_id={"win": o},
        )

    def along_remote(t, piece):
        owner = (me_w - t + N_WIN) % N_WIN
        return pltpu.make_async_remote_copy(
            src_ref=piece,
            dst_ref=lag_recv.at[z],
            send_sem=f_send.at[t],
            recv_sem=f_recv.at[z],
            device_id={"pair": x * NZ + owner},
        )

    def along(t, piece):
        owner = (me_w - t + N_WIN) % N_WIN

        @pl.when(owner == z)
        def _():
            pltpu.make_async_copy(piece, lag_recv.at[z], f_recv.at[z]).start()

        @pl.when(owner != z)
        def _():
            along_remote(t, piece).start()

    HOPS = (4, 3, 5, 2, 6, 1, 7)
    for t in HOPS:
        across(t).start()
    along(0, lag_send.at[me_w])
    for t in HOPS[::-1]:
        across(t).wait_recv()
        along(t, lag_held.at[t])

    counts = []
    for j in range(PC // N_WIN):
        count = jnp.zeros((PR, 128), f32)
        for w in range(N_WIN):
            column = pl.ds(NEED * w + PR + (PC // N_WIN) * me_w + j, 1)
            count = count + final_present[NEED * w : NEED * w + PR, :] * final_present[column, :]
        counts.append(count)
    count = jnp.maximum(jnp.concatenate(counts, axis=0)[:, :1], 1.0)

    total = jnp.zeros((SHARE, LAGS), f32)
    for k in range(NZ):
        piece = lag_recv.at[k]
        pltpu.make_async_copy(piece, piece, f_recv.at[k]).wait()
        total = total + lag_recv[k].astype(f32)
    out_ref[...] = total / count

    for s in range(STEPS):
        sent = recv1.at[s, pl.ds(0, NZ - 1)]
        pltpu.make_async_copy(sent, sent, d_send.at[s]).wait()
        sent = send2.at[s, pl.ds(0, PLANE - 1)]
        pltpu.make_async_copy(sent, sent, s_send.at[s]).wait()
    pltpu.make_async_copy(near_masks, near_masks, m_send.at[0]).wait()
    pltpu.make_async_copy(far_masks, far_masks, m_send.at[1]).wait()
    for t in range(1, N_WIN):
        across(t).wait_send()
    for t in range(N_WIN):

        @pl.when((me_w - t + N_WIN) % N_WIN != z)
        def _(t=t):
            along_remote(t, lag_send.at[0]).wait_send()


def per_device(spectra, availability, owners):
    dma = pltpu.SemaphoreType.DMA
    anywhere = pl.BlockSpec(memory_space=pl.ANY)
    out = pl.pallas_call(
        kernel,
        out_shape=jax.ShapeDtypeStruct((SHARE, LAGS), f32),
        in_specs=[anywhere] * 3,
        out_specs=pl.BlockSpec(memory_space=pltpu.VMEM),
        scratch_shapes=[
            pltpu.VMEM((BLOCK, 2, BINS), bf16),
            pltpu.VMEM((N_PAIR, NEED), i32),
            pltpu.VMEM((1, BLOCK), i32),
            pltpu.VMEM((STEPS, NZ, BLOCK, 2, SUB), bf16),
            pltpu.VMEM((STEPS, N_PAIR, MSG, SUB), bf16),
            pltpu.VMEM((STEPS, PLANE, MSG, SUB), bf16),
            pltpu.VMEM((STEPS, 2 * SUB, LAGS), bf16),
            pltpu.VMEM((N_WIN, 2, NEED, SUB), f32),
            pltpu.VMEM((2 * PAIRS, 2 * SUB), bf16),
            pltpu.VMEM((PAIRS, LAGS), f32),
            pltpu.VMEM((HALVES, 16 * N_PAIR, QUAD * 2 * BLOCK), bf16),
            pltpu.VMEM((CHUNK // FINE, LAGS), f32),
            pltpu.VMEM((CHUNK // FINE, LAGS), f32),
            pltpu.VMEM((NZ, 1, 128), f32),
            pltpu.VMEM((N_WIN * N_PAIR, 1, 128), f32),
            pltpu.VMEM((N_WIN * NEED, 128), f32),
            pltpu.VMEM((N_WIN * NEED, 128), f32),
            pltpu.VMEM((N_WIN, SHARE, LAGS), bf16),
            pltpu.VMEM((N_WIN, SHARE, LAGS), bf16),
            pltpu.VMEM((NZ, SHARE, LAGS), bf16),
            dma((3,)),
            dma((STEPS,)),
            dma((STEPS,)),
            dma((STEPS,)),
            dma((STEPS,)),
            dma((2,)),
            dma((2,)),
            dma((N_WIN,)),
            dma((N_WIN,)),
            dma((N_WIN,)),
            dma((NZ,)),
        ],
        compiler_params=pltpu.CompilerParams(
            collective_id=0, has_side_effects=True, vmem_limit_bytes=48 * 1024 * 1024
        ),
        cost_estimate=pl.CostEstimate(
            flops=6_000_000_000, bytes_accessed=2_000_000, transcendentals=1_000_000
        ),
    )(spectra, owners, availability)
    return out.reshape(PC // N_WIN, PR, LAGS)


def solution(mesh):
    return jax.shard_map(
        per_device,
        mesh=mesh,
        in_specs=(P("win", "pair", None, None), P("win", "pair"), P()),
        out_specs=P("win", "pair", None),
        check_vma=False,
    )
```

time: 320 us -> 61.3 us (0.19)
  the two profiles are of different devices: /device:TPU:1 before, /device:TPU:16 now
where the time goes in v2:
time: 61.3 us; the launch traced here: 61.1 us
  Pallas kernels  57.9 us (94%)
  local copies, waits for them, and re-layouts  3.23 us (5%)
    pallas_call x1, Pallas kernels, per_device(): pl.pallas_call(kernel, out_shape=jax.ShapeDtypeStruct((SHARE, LAGS), f32)...  57.9 us
    unnamed x7, local copies, waits for them, and re-layouts  3.23 us

profile of v2, /device:TPU:16, one launch (start us, length us, event | category | flops | bytes accessed | tf_op | source)
XLA Modules:
  0.0 61.1 jit_solution(6020349807453200972)
XLA Ops:
  0.0 0.0 copy-start
  0.0 1.2 %copy-done = bf16[1,32,2,8192]{3,2,1,0:T(2,128)(2,1)S(1)} copy-done((bf16[1,32,2,8192]{3,2,1,0:T(2,128)(2,1)S(1)}, bf16[1,32,2,8192]{3,2,1,0:T(2,128)(2,1)}, u32[]{:S(2)}) %copy-start) | copy-done | bytes 1048600
  1.2 0.0 copy-start.1
  1.2 0.7 %copy-done.1 = s32[32,32]{1,0:T(8,128)S(1)} copy-done((s32[32,32]{1,0:T(8,128)S(1)}, s32[32,32]{1,0:T(8,128)}, u32[]{:S(2)}) %copy-start.1) | copy-done | bytes 4120
  1.9 0.0 copy-start.2
  1.9 0.7 %copy-done.2 = s32[1,32]{1,0:T(1,128)S(1)} copy-done((s32[1,32]{1,0:T(1,128)S(1)}, s32[1,32]{1,0:T(1,128)}, u32[]{:S(2)}) %copy-start.2) | copy-done | bytes 152
  2.6 57.9 %shard_map.37 = f32[32,512]{1,0:T(8,128)S(1)} custom-call(bf16[1,32,2,8192]{3,2,1,0:T(2,128)(2,1)S(1)} %copy-done, s32[32,32]{1,0:T(8,128)S(1)} %copy-done.1, s32[1,32]{1,0:T(1,128)S(1)} %copy-done.2), custom_call_target="tpu_custom_call" | custom-call | flops 6000000000 | bytes 2000000 | tf_op jit(solution)/shard_map/pallas_call | solution.py:369
  60.5 0.6 %copy.5 = f32[2,16,512]{2,1,0:T(8,128)} copy(f32[2,16,512]{2,1,0:T(8,128)S(1)} %bitcast.1) | data formatting | bytes 131072
Async XLA Ops:
  0.0 1.2 %copy-start = (bf16[1,32,2,8192]{3,2,1,0:T(2,128)(2,1)S(1)}, bf16[1,32,2,8192]{3,2,1,0:T(2,128)(2,1)}, u32[]{:S(2)}) copy-start(bf16[1,32,2,8192]{3,2,1,0:T(2,128)(2,1)} %x_hbm.1) | copy-start | bytes 3145732
  1.2 0.7 %copy-start.1 = (s32[32,32]{1,0:T(8,128)S(1)}, s32[32,32]{1,0:T(8,128)}, u32[]{:S(2)}) copy-start(s32[32,32]{1,0:T(8,128)} %own_hbm.1) | copy-start | bytes 12292
  1.9 0.7 %copy-start.2 = (s32[1,32]{1,0:T(1,128)S(1)}, s32[1,32]{1,0:T(1,128)}, u32[]{:S(2)}) copy-start(s32[1,32]{1,0:T(1,128)} %avail_hbm.1) | copy-start | bytes 388

commit v3 on v2

v3 whole, which is shorter than its diff:
```python
import math

import jax
import jax.numpy as jnp
from jax import lax
from jax.experimental import pallas as pl
from jax.experimental.pallas import tpu as pltpu
from jax.sharding import PartitionSpec as P

WB = 64
LAGS = 512
PR = 16
PC = 16
NEED = 32
EPSILON = 1e-06

NX, NZ = 4, 8
N_PAIR = NX * NZ
N_WIN = 8
BLOCK = 32
BINS = 8192
CHUNK = BINS // NZ
WIDTHS = (256, 256, 256, 256)
STEPS = len(WIDTHS)
STARTS = tuple(sum(WIDTHS[:s]) for s in range(STEPS))
WIDEST = max(WIDTHS)
AHEAD = 2
PLANE = NX * N_WIN
HALVES = 2
QUAD = NZ // HALVES
MSG = 4 * NZ
PERIOD = 2 * BINS
FINE = 32
PAIRS = PC * PR
SHARE = PAIRS // N_WIN

f32 = jnp.float32
bf16 = jnp.bfloat16
i32 = jnp.int32

Z_OFFSETS = [4, 3, -3, 2, -2, 1, -1]
PLANE_OFFSETS = [(dw, dx) for dw in (4, 3, 5, 2, 6, 1, 7, 0) for dx in (2, 1, -1, 0)][:-1]


def iota(shape, dim):
    return lax.broadcasted_iota(i32, shape, dim)


def work_z(w, z):
    y, core = w // 2, w % 2
    near = jnp.where(y < 2, 4 - 2 * y, 3 - 2 * ((y + z) % 2))
    return (z + near + 4 * core) % NZ


def worker(offset, z):
    core = 0 if 1 <= offset <= 4 else 1
    near = offset - 4 * core
    near = near + NZ if near < 0 else near
    odd = z % 2
    y = {4: 0, 2: 1, 3: 2 + odd, 1: 3 - odd}[near]
    return 2 * y + core


def kernel(
    x_hbm,
    own_hbm,
    avail_hbm,
    out_ref,
    x_ref,
    own_ref,
    avail_ref,
    white,
    lhs,
    acc,
    smat,
    cos_a,
    sin_a,
    mask_z,
    mask_all,
    present,
    final_present,
    lag_send,
    lag_recv,
    in_sem,
    d_send,
    d_recv,
    s_send,
    s_recv,
    m_send,
    m_recv,
    l_send,
    l_recv,
    *steps,
):
    recv1, send2, recv2, table = (steps[STEPS * i : STEPS * (i + 1)] for i in range(4))
    me_w = lax.axis_index("win")
    me_p = lax.axis_index("pair")
    x, z = me_p // NZ, me_p % NZ
    z_peers = [(z + dz + NZ) % NZ for dz in Z_OFFSETS]
    my_owner_z = work_z(me_w, z)
    plane_peers = [((me_w + dw) % N_WIN, (x + dx + NX) % NX) for dw, dx in PLANE_OFFSETS]

    barrier = pltpu.get_barrier_semaphore()
    for k in z_peers:
        pl.semaphore_signal(barrier, inc=1, device_id={"pair": x * NZ + k})
    for o, k in plane_peers:
        pl.semaphore_signal(barrier, inc=1, device_id={"win": o, "pair": k * NZ + z})
    for offset in range(1, NZ):
        k = (z - offset + NZ) % NZ
        pl.semaphore_signal(
            barrier, inc=1, device_id={"win": worker(offset, k), "pair": x * NZ + k}
        )
    own_in = pltpu.make_async_copy(own_hbm, own_ref, in_sem.at[0])
    avail_in = pltpu.make_async_copy(avail_hbm, avail_ref, in_sem.at[1])
    x_in = pltpu.make_async_copy(x_hbm.at[0], x_ref, in_sem.at[2])
    own_in.start()
    avail_in.start()
    x_in.start()
    avail_in.wait()
    mask_z[z] = jnp.concatenate(
        [avail_ref[...].astype(f32), jnp.zeros((1, 128 - BLOCK), f32)], axis=1
    )
    x_in.wait()
    pl.semaphore_wait(barrier, NZ - 1 + PLANE - 1 + jnp.where(me_w == 1, 0, N_WIN))


    def spectra_step(s, k):
        bins = pl.ds(pl.multiple_of(k * CHUNK + STARTS[s], 128), WIDTHS[s])
        return x_ref.at[:, :, bins]

    def start_spectra(s):
        for k in z_peers:
            pltpu.make_async_remote_copy(
                src_ref=spectra_step(s, k),
                dst_ref=recv1[s].at[z],
                send_sem=d_send.at[s],
                recv_sem=d_recv.at[s],
                device_id={"pair": x * NZ + k},
            ).start()
        pltpu.make_async_copy(spectra_step(s, z), recv1[s].at[z], d_recv.at[s]).start()

    for k in z_peers:
        pltpu.make_async_remote_copy(
            src_ref=mask_z.at[z],
            dst_ref=mask_z.at[z],
            send_sem=m_send.at[0],
            recv_sem=m_recv.at[0],
            device_id={"pair": x * NZ + k},
        ).start()

    for s in range(AHEAD):
        start_spectra(s)
    own_in.wait()

    rows = 16 * N_PAIR
    owners = own_ref[...]
    spread = (iota((rows, N_PAIR), 0) >> 4 == iota((rows, N_PAIR), 1)).astype(bf16)
    block = jnp.dot(spread, (owners >> 5).astype(bf16), preferred_element_type=f32)
    station = jnp.dot(spread, (owners & 31).astype(bf16), preferred_element_type=f32)
    row = iota((rows, 1), 0)
    near = (row >> 2) & 3
    upper_slot = ((row >> 1) & 1) == 1
    for half in range(HALVES):
        mine = block == (x * NZ + half * QUAD + near).astype(f32)
        first = jnp.min(jnp.where(mine, station, BLOCK - 1.0), axis=1, keepdims=True)
        last = jnp.max(jnp.where(mine, station, 0.0), axis=1, keepdims=True)
        wanted = jnp.where(upper_slot, last, first).astype(i32)
        source = near * (2 * BLOCK) + 2 * wanted + (row & 1)
        smat[half] = (iota((rows, QUAD * 2 * BLOCK), 1) == source).astype(bf16)

    near_masks = mask_z.at[pl.ds(0, NZ - 1)]
    pltpu.make_async_copy(near_masks, near_masks, m_recv.at[0]).wait()
    here = pl.ds((me_w * NX + x) * NZ, NZ)
    for o, k in plane_peers:
        pltpu.make_async_remote_copy(
            src_ref=mask_z,
            dst_ref=mask_all.at[here],
            send_sem=m_send.at[1],
            recv_sem=m_recv.at[1],
            device_id={"win": o, "pair": k * NZ + z},
        ).start()
    mask_all[here] = mask_z[...]
    far_masks = mask_all.at[pl.ds(0, N_WIN * N_PAIR - NZ)]

    def relay(s):
        whole = recv1[s]
        pltpu.make_async_copy(whole, whole, d_recv.at[s]).wait()

        if s + AHEAD < STEPS:
            start_spectra(s + AHEAD)

        for half in range(HALVES):
            stations = recv1[s][half * QUAD : (half + 1) * QUAD]
            stations = stations.reshape(QUAD * 2 * BLOCK, WIDTHS[s])
            message = jnp.dot(smat[half], stations, preferred_element_type=f32).astype(bf16)
            send2[s][:, 16 * half : 16 * (half + 1), :] = message.reshape(N_PAIR, 16, WIDTHS[s])
        for o, k in plane_peers:
            pltpu.make_async_remote_copy(
                src_ref=send2[s].at[k * NZ + work_z(o, z)],
                dst_ref=recv2[s].at[me_w * NX + x],
                send_sem=s_send.at[s],
                recv_sem=s_recv.at[s],
                device_id={"win": o, "pair": k * NZ + z},
            ).start()
        recv2[s][me_w * NX + x] = send2[s][x * NZ + my_owner_z]

    def process(s):
        wide = WIDTHS[s]
        others = recv2[s].at[pl.ds(0, PLANE - 1)]
        pltpu.make_async_copy(others, others, s_recv.at[s]).wait()
        for w in range(N_WIN):
            messages = recv2[s][NX * w : NX * (w + 1)].reshape(NX * MSG, wide)
            lines = jnp.dot(rmat, messages, preferred_element_type=f32)
            re, im = lines[:NEED], lines[NEED:]
            magnitude = jnp.sqrt(re * re + im * im)
            upper = magnitude.astype(bf16)
            lower = (magnitude - upper.astype(f32)).astype(bf16)
            level = jnp.dot(upper, band[:wide, :wide], preferred_element_type=f32) + jnp.dot(
                lower, band[:wide, :wide], preferred_element_type=f32
            )
            factor = present[NEED * w : NEED * (w + 1), :1] / (level + EPSILON)
            white[w, 0, :, :wide] = (re * factor).astype(bf16).astype(f32)
            white[w, 1, :, :wide] = (im * factor).astype(bf16).astype(f32)
        for j in range(PC):
            total_re = jnp.zeros((PR, wide), f32)
            total_im = jnp.zeros((PR, wide), f32)
            for w in range(N_WIN):
                ar, ai = white[w, 0, :PR, :wide], white[w, 1, :PR, :wide]
                br = white[w, 0, PR + j : PR + j + 1, :wide]
                bi = white[w, 1, PR + j : PR + j + 1, :wide]
                total_re = total_re + (ar * br + ai * bi)
                total_im = total_im + (ai * br - ar * bi)
            for part, total in enumerate((total_re, total_im)):
                upper = total.astype(bf16)
                lower = (total - upper.astype(f32)).astype(bf16)
                lhs[PR * j : PR * (j + 1), wide * part : wide * (part + 1)] = upper
                lhs[PAIRS + PR * j : PAIRS + PR * (j + 1), wide * part : wide * (part + 1)] = lower
        product = jnp.dot(lhs[:, : 2 * wide], table[s][...], preferred_element_type=f32)
        acc[...] += product[:PAIRS] + product[PAIRS:]

    relay(0)

    lag = iota((FINE, LAGS), 1) - LAGS // 2
    index = iota((FINE, LAGS), 0)

    def angle(phase):
        phase = ((phase + PERIOD // 2) & (PERIOD - 1)) - PERIOD // 2
        return phase.astype(f32) * (2.0 * math.pi / PERIOD)

    coarse = angle((z * CHUNK + FINE * index) * lag)
    cos_a[...] = jnp.cos(coarse)
    sin_a[...] = jnp.sin(coarse)
    fine = angle(index * lag)
    cos_b, sin_b = jnp.cos(fine), jnp.sin(fine)

    for s in range(STEPS):

        def table_rows(n, carry, s=s):
            at = STARTS[s] // FINE + n
            ca, sa = cos_a[pl.ds(at, 1), :], sin_a[pl.ds(at, 1), :]
            bins = z * CHUNK + FINE * at + iota((FINE, 1), 0)
            weight = jnp.where(bins == 0, 1.0, 2.0) / math.sqrt(PERIOD)
            real = pl.ds(pl.multiple_of(n * FINE, FINE), FINE)
            imag = pl.ds(pl.multiple_of(WIDTHS[s] + n * FINE, FINE), FINE)
            table[s][real, :] = (weight * (ca * cos_b - sa * sin_b)).astype(bf16)
            table[s][imag, :] = (-weight * (sa * cos_b + ca * sin_b)).astype(bf16)
            return carry

        lax.fori_loop(0, WIDTHS[s] // FINE, table_rows, 0)

    def pick(count, lane, own_row):
        hit = iota((count, NEED), 1) == lane
        return jnp.sum(jnp.where(hit, own_row, 0), axis=1, keepdims=True)

    work_row = own_ref[pl.ds(x * NZ + my_owner_z, 1), :]
    sel = iota((2 * NEED, 1), 0)
    chosen = pick(2 * NEED, sel & (NEED - 1), work_row)
    earlier = jnp.logical_and(work_row >> 5 == chosen >> 5, work_row < chosen)
    slot = jnp.max(earlier.astype(f32), axis=1, keepdims=True).astype(i32)
    target = (chosen >> 5) * 4 + slot * 2 + (sel >> 5)
    rmat = (iota((2 * NEED, NX * MSG), 1) == target).astype(bf16)
    band = jnp.where(iota((WIDEST, WIDEST), 0) >> 6 == iota((WIDEST, WIDEST), 1) >> 6, 1.0 / WB, 0.0)
    band = band.astype(bf16)
    acc[...] = jnp.zeros_like(acc)

    line = iota((N_WIN * NEED, 1), 0)

    def availability_of(masks, own_row):
        who = pick(N_WIN * NEED, line & (NEED - 1), own_row)
        place = (line >> 5) * N_PAIR + (who >> 5)
        where = (iota((N_WIN * NEED, N_WIN * N_PAIR), 1) == place).astype(bf16)
        found = jnp.dot(where, masks, preferred_element_type=f32)
        hit = iota((N_WIN * NEED, 128), 1) == who & 31
        value = jnp.sum(jnp.where(hit, found, 0.0), axis=1, keepdims=True)
        return jnp.broadcast_to(value, (N_WIN * NEED, 128))


    relay(1)
    pltpu.make_async_copy(far_masks, far_masks, m_recv.at[1]).wait()
    masks = mask_all[:, 0, :].astype(bf16)
    present[...] = availability_of(masks, work_row)
    final_present[...] = availability_of(masks, own_ref[pl.ds(me_p, 1), :])
    process(0)
    for s in range(2, STEPS):
        relay(s)
        process(s - 1)
    process(STEPS - 1)

    lag_send[...] = acc[...].astype(bf16).reshape(N_WIN, SHARE, LAGS)

    def lagged(t):
        o = (me_w + t) % N_WIN
        return pltpu.make_async_remote_copy(
            src_ref=lag_send.at[o],
            dst_ref=lag_recv.at[z],
            send_sem=l_send.at[t],
            recv_sem=l_recv.at[z],
            device_id={"win": o, "pair": x * NZ + my_owner_z},
        )

    for t in (4, 3, 5, 2, 6, 1, 7):
        lagged(t).start()

    @pl.when(me_w == 1)
    def _():
        pltpu.make_async_copy(lag_send.at[me_w], lag_recv.at[z], l_recv.at[z]).start()

    @pl.when(me_w != 1)
    def _():
        lagged(0).start()

    counts = []
    for j in range(PC // N_WIN):
        count = jnp.zeros((PR, 128), f32)
        for w in range(N_WIN):
            column = pl.ds(NEED * w + PR + (PC // N_WIN) * me_w + j, 1)
            count = count + final_present[NEED * w : NEED * w + PR, :] * final_present[column, :]
        counts.append(count)
    count = jnp.maximum(jnp.concatenate(counts, axis=0)[:, :1], 1.0)

    total = jnp.zeros((SHARE, LAGS), f32)
    for k in range(NZ):
        piece = lag_recv.at[k]
        pltpu.make_async_copy(piece, piece, l_recv.at[k]).wait()
        total = total + lag_recv[k].astype(f32)
    out_ref[...] = total / count

    for s in range(STEPS):
        sent = recv1[s].at[pl.ds(0, NZ - 1)]
        pltpu.make_async_copy(sent, sent, d_send.at[s]).wait()
        sent = send2[s].at[pl.ds(0, PLANE - 1)]
        pltpu.make_async_copy(sent, sent, s_send.at[s]).wait()
    pltpu.make_async_copy(near_masks, near_masks, m_send.at[0]).wait()
    pltpu.make_async_copy(far_masks, far_masks, m_send.at[1]).wait()
    for t in range(1, N_WIN):
        lagged(t).wait_send()

    @pl.when(me_w != 1)
    def _():
        lagged(0).wait_send()


def per_device(spectra, availability, owners):
    dma = pltpu.SemaphoreType.DMA
    anywhere = pl.BlockSpec(memory_space=pl.ANY)
    out = pl.pallas_call(
        kernel,
        out_shape=jax.ShapeDtypeStruct((SHARE, LAGS), f32),
        in_specs=[anywhere] * 3,
        out_specs=pl.BlockSpec(memory_space=pltpu.VMEM),
        scratch_shapes=[
            pltpu.VMEM((BLOCK, 2, BINS), bf16),
            pltpu.VMEM((N_PAIR, NEED), i32),
            pltpu.VMEM((1, BLOCK), i32),
            pltpu.VMEM((N_WIN, 2, NEED, WIDEST), f32),
            pltpu.VMEM((2 * PAIRS, 2 * WIDEST), bf16),
            pltpu.VMEM((PAIRS, LAGS), f32),
            pltpu.VMEM((HALVES, 16 * N_PAIR, QUAD * 2 * BLOCK), bf16),
            pltpu.VMEM((CHUNK // FINE, LAGS), f32),
            pltpu.VMEM((CHUNK // FINE, LAGS), f32),
            pltpu.VMEM((NZ, 1, 128), f32),
            pltpu.VMEM((N_WIN * N_PAIR, 1, 128), f32),
            pltpu.VMEM((N_WIN * NEED, 128), f32),
            pltpu.VMEM((N_WIN * NEED, 128), f32),
            pltpu.VMEM((N_WIN, SHARE, LAGS), bf16),
            pltpu.VMEM((NZ, SHARE, LAGS), bf16),
            dma((3,)),
            dma((STEPS,)),
            dma((STEPS,)),
            dma((STEPS,)),
            dma((STEPS,)),
            dma((2,)),
            dma((2,)),
            dma((N_WIN,)),
            dma((NZ,)),
        ]
        + [pltpu.VMEM((NZ, BLOCK, 2, wide), bf16) for wide in WIDTHS]
        + [pltpu.VMEM((N_PAIR, MSG, wide), bf16) for wide in WIDTHS]
        + [pltpu.VMEM((PLANE, MSG, wide), bf16) for wide in WIDTHS]
        + [pltpu.VMEM((2 * wide, LAGS), bf16) for wide in WIDTHS],
        compiler_params=pltpu.CompilerParams(
            collective_id=0, has_side_effects=True, vmem_limit_bytes=48 * 1024 * 1024
        ),
        cost_estimate=pl.CostEstimate(
            flops=6_000_000_000, bytes_accessed=2_000_000, transcendentals=1_000_000
        ),
    )(spectra, owners, availability)
    return out.reshape(PC // N_WIN, PR, LAGS)


def solution(mesh):
    return jax.shard_map(
        per_device,
        mesh=mesh,
        in_specs=(P("win", "pair", None, None), P("win", "pair"), P()),
        out_specs=P("win", "pair", None),
        check_vma=False,
    )
```

time: 61.3 us -> 58.1 us (0.948)
  the two profiles are of different devices: /device:TPU:16 before, /device:TPU:1 now
where the time goes in v3:
time: 58.1 us; the launch traced here: 57.9 us
  Pallas kernels  54.7 us (94%)
  local copies, waits for them, and re-layouts  3.23 us (6%)
    pallas_call x1, Pallas kernels, per_device(): pl.pallas_call(kernel, out_shape=jax.ShapeDtypeStruct((SHARE, LAGS), f32)...  54.7 us
    unnamed x7, local copies, waits for them, and re-layouts  3.23 us

profile of v3, /device:TPU:1, one launch (start us, length us, event | category | flops | bytes accessed | tf_op | source)
XLA Modules:
  0.0 57.9 jit_solution(17723962401614652412)
XLA Ops:
  0.0 0.0 copy-start
  0.0 1.2 %copy-done = bf16[1,32,2,8192]{3,2,1,0:T(2,128)(2,1)S(1)} copy-done((bf16[1,32,2,8192]{3,2,1,0:T(2,128)(2,1)S(1)}, bf16[1,32,2,8192]{3,2,1,0:T(2,128)(2,1)}, u32[]{:S(2)}) %copy-start) | copy-done | bytes 1048600
  1.2 0.0 copy-start.1
  1.2 0.7 %copy-done.1 = s32[32,32]{1,0:T(8,128)S(1)} copy-done((s32[32,32]{1,0:T(8,128)S(1)}, s32[32,32]{1,0:T(8,128)}, u32[]{:S(2)}) %copy-start.1) | copy-done | bytes 4120
  1.9 0.0 copy-start.2
  1.9 0.7 %copy-done.2 = s32[1,32]{1,0:T(1,128)S(1)} copy-done((s32[1,32]{1,0:T(1,128)S(1)}, s32[1,32]{1,0:T(1,128)}, u32[]{:S(2)}) %copy-start.2) | copy-done | bytes 152
  2.6 54.7 %shard_map.37 = f32[32,512]{1,0:T(8,128)S(1)} custom-call(bf16[1,32,2,8192]{3,2,1,0:T(2,128)(2,1)S(1)} %copy-done, s32[32,32]{1,0:T(8,128)S(1)} %copy-done.1, s32[1,32]{1,0:T(1,128)S(1)} %copy-done.2), custom_call_target="tpu_custom_call" | custom-call | flops 6000000000 | bytes 2000000 | tf_op jit(solution)/shard_map/pallas_call | solution.py:366
  57.3 0.6 %copy.5 = f32[2,16,512]{2,1,0:T(8,128)} copy(f32[2,16,512]{2,1,0:T(8,128)S(1)} %bitcast.1) | data formatting | bytes 131072
Async XLA Ops:
  0.0 1.2 %copy-start = (bf16[1,32,2,8192]{3,2,1,0:T(2,128)(2,1)S(1)}, bf16[1,32,2,8192]{3,2,1,0:T(2,128)(2,1)}, u32[]{:S(2)}) copy-start(bf16[1,32,2,8192]{3,2,1,0:T(2,128)(2,1)} %x_hbm.1) | copy-start | bytes 3145732
  1.2 0.7 %copy-start.1 = (s32[32,32]{1,0:T(8,128)S(1)}, s32[32,32]{1,0:T(8,128)}, u32[]{:S(2)}) copy-start(s32[32,32]{1,0:T(8,128)} %own_hbm.1) | copy-start | bytes 12292
  1.9 0.7 %copy-start.2 = (s32[1,32]{1,0:T(1,128)S(1)}, s32[1,32]{1,0:T(1,128)}, u32[]{:S(2)}) copy-start(s32[1,32]{1,0:T(1,128)} %avail_hbm.1) | copy-start | bytes 388

commit v4 on v3

--- a/solution.py
+++ b/solution.py
@@ -20,11 +20,11 @@
 BLOCK = 32
 BINS = 8192
 CHUNK = BINS // NZ
-WIDTHS = (256, 256, 256, 256)
+WIDTHS = (128,) * 8
 STEPS = len(WIDTHS)
 STARTS = tuple(sum(WIDTHS[:s]) for s in range(STEPS))
 WIDEST = max(WIDTHS)
-AHEAD = 2
+AHEAD = 3
 PLANE = NX * N_WIN
 HALVES = 2
 QUAD = NZ // HALVES
@@ -208,19 +208,24 @@
         wide = WIDTHS[s]
         others = recv2[s].at[pl.ds(0, PLANE - 1)]
         pltpu.make_async_copy(others, others, s_recv.at[s]).wait()
+        res, ims, magnitudes = [], [], []
         for w in range(N_WIN):
             messages = recv2[s][NX * w : NX * (w + 1)].reshape(NX * MSG, wide)
             lines = jnp.dot(rmat, messages, preferred_element_type=f32)
-            re, im = lines[:NEED], lines[NEED:]
-            magnitude = jnp.sqrt(re * re + im * im)
-            upper = magnitude.astype(bf16)
-            lower = (magnitude - upper.astype(f32)).astype(bf16)
-            level = jnp.dot(upper, band[:wide, :wide], preferred_element_type=f32) + jnp.dot(
-                lower, band[:wide, :wide], preferred_element_type=f32
-            )
-            factor = present[NEED * w : NEED * (w + 1), :1] / (level + EPSILON)
-            white[w, 0, :, :wide] = (re * factor).astype(bf16).astype(f32)
-            white[w, 1, :, :wide] = (im * factor).astype(bf16).astype(f32)
+            res.append(lines[:NEED])
+            ims.append(lines[NEED:])
+            magnitudes.append(jnp.sqrt(res[w] * res[w] + ims[w] * ims[w]))
+        magnitude = jnp.concatenate(magnitudes, axis=0)
+        upper = magnitude.astype(bf16)
+        lower = (magnitude - upper.astype(f32)).astype(bf16)
+        both = jnp.concatenate([upper, lower], axis=0)
+        levels = jnp.dot(both, band[:wide, :wide], preferred_element_type=f32)
+        level = levels[: N_WIN * NEED] + levels[N_WIN * NEED :]
+        factor = present[:, :1] / (level + EPSILON)
+        for w in range(N_WIN):
+            own = factor[NEED * w : NEED * (w + 1)]
+            white[w, 0, :, :wide] = (res[w] * own).astype(bf16).astype(f32)
+            white[w, 1, :, :wide] = (ims[w] * own).astype(bf16).astype(f32)
         for j in range(PC):
             total_re = jnp.zeros((PR, wide), f32)
             total_im = jnp.zeros((PR, wide), f32)
@@ -300,11 +305,11 @@
     masks = mask_all[:, 0, :].astype(bf16)
     present[...] = availability_of(masks, work_row)
     final_present[...] = availability_of(masks, own_ref[pl.ds(me_p, 1), :])
-    process(0)
     for s in range(2, STEPS):
         relay(s)
-        process(s - 1)
-    process(STEPS - 1)
+        process(s - 2)
+    for s in range(STEPS - 2, STEPS):
+        process(s)
 
     lag_send[...] = acc[...].astype(bf16).reshape(N_WIN, SHARE, LAGS)
 

time: 58.1 us -> 57.2 us (0.985)
  Pallas kernels: 54.7 us -> 53.8 us
    pallas_call x1, Pallas kernels: 54.7 us -> 53.8 us  [per_device(): pl.pallas_call(kernel, out_shape=jax.ShapeDtypeStruct((SHARE, LAGS), f32)...]
where the time goes in v4:
time: 57.2 us; the launch traced here: 57.1 us
  Pallas kernels  53.8 us (94%)
  local copies, waits for them, and re-layouts  3.23 us (6%)
    pallas_call x1, Pallas kernels, per_device(): pl.pallas_call(kernel, out_shape=jax.ShapeDtypeStruct((SHARE, LAGS), f32)...  53.8 us
    unnamed x7, local copies, waits for them, and re-layouts  3.23 us

profile of v4, /device:TPU:1, one launch (start us, length us, event | category | flops | bytes accessed | tf_op | source)
XLA Modules:
  0.0 57.1 jit_solution(3816073675274233151)
XLA Ops:
  0.0 0.0 copy-start
  0.0 1.2 %copy-done = bf16[1,32,2,8192]{3,2,1,0:T(2,128)(2,1)S(1)} copy-done((bf16[1,32,2,8192]{3,2,1,0:T(2,128)(2,1)S(1)}, bf16[1,32,2,8192]{3,2,1,0:T(2,128)(2,1)}, u32[]{:S(2)}) %copy-start) | copy-done | bytes 1048600
  1.2 0.0 copy-start.1
  1.2 0.7 %copy-done.1 = s32[32,32]{1,0:T(8,128)S(1)} copy-done((s32[32,32]{1,0:T(8,128)S(1)}, s32[32,32]{1,0:T(8,128)}, u32[]{:S(2)}) %copy-start.1) | copy-done | bytes 4120
  1.9 0.0 copy-start.2
  1.9 0.7 %copy-done.2 = s32[1,32]{1,0:T(1,128)S(1)} copy-done((s32[1,32]{1,0:T(1,128)S(1)}, s32[1,32]{1,0:T(1,128)}, u32[]{:S(2)}) %copy-start.2) | copy-done | bytes 152
  2.6 53.8 %shard_map.37 = f32[32,512]{1,0:T(8,128)S(1)} custom-call(bf16[1,32,2,8192]{3,2,1,0:T(2,128)(2,1)S(1)} %copy-done, s32[32,32]{1,0:T(8,128)S(1)} %copy-done.1, s32[1,32]{1,0:T(1,128)S(1)} %copy-done.2), custom_call_target="tpu_custom_call" | custom-call | flops 6000000000 | bytes 2000000 | tf_op jit(solution)/shard_map/pallas_call | solution.py:371
  56.4 0.6 %copy.5 = f32[2,16,512]{2,1,0:T(8,128)} copy(f32[2,16,512]{2,1,0:T(8,128)S(1)} %bitcast.1) | data formatting | bytes 131072
Async XLA Ops:
  0.0 1.2 %copy-start = (bf16[1,32,2,8192]{3,2,1,0:T(2,128)(2,1)S(1)}, bf16[1,32,2,8192]{3,2,1,0:T(2,128)(2,1)}, u32[]{:S(2)}) copy-start(bf16[1,32,2,8192]{3,2,1,0:T(2,128)(2,1)} %x_hbm.1) | copy-start | bytes 3145732
  1.2 0.7 %copy-start.1 = (s32[32,32]{1,0:T(8,128)S(1)}, s32[32,32]{1,0:T(8,128)}, u32[]{:S(2)}) copy-start(s32[32,32]{1,0:T(8,128)} %own_hbm.1) | copy-start | bytes 12292
  1.9 0.7 %copy-start.2 = (s32[1,32]{1,0:T(1,128)S(1)}, s32[1,32]{1,0:T(1,128)}, u32[]{:S(2)}) copy-start(s32[1,32]{1,0:T(1,128)} %avail_hbm.1) | copy-start | bytes 388

commit v5 on v4

--- a/solution.py
+++ b/solution.py
@@ -307,8 +307,9 @@
     final_present[...] = availability_of(masks, own_ref[pl.ds(me_p, 1), :])
     for s in range(2, STEPS):
         relay(s)
-        process(s - 2)
-    for s in range(STEPS - 2, STEPS):
+        if s >= 3:
+            process(s - 3)
+    for s in range(STEPS - 3, STEPS):
         process(s)
 
     lag_send[...] = acc[...].astype(bf16).reshape(N_WIN, SHARE, LAGS)

time: 57.2 us -> 56 us (0.979)
  Pallas kernels: 53.8 us -> 52.6 us
    pallas_call x1, Pallas kernels: 53.8 us -> 52.6 us  [per_device(): pl.pallas_call(kernel, out_shape=jax.ShapeDtypeStruct((SHARE, LAGS), f32)...]
where the time goes in v5:
time: 56 us; the launch traced here: 55.8 us
  Pallas kernels  52.6 us (94%)
  local copies, waits for them, and re-layouts  3.23 us (6%)
    pallas_call x1, Pallas kernels, per_device(): pl.pallas_call(kernel, out_shape=jax.ShapeDtypeStruct((SHARE, LAGS), f32)...  52.6 us
    unnamed x7, local copies, waits for them, and re-layouts  3.23 us

profile of v5, /device:TPU:1, one launch (start us, length us, event | category | flops | bytes accessed | tf_op | source)
XLA Modules:
  0.0 55.8 jit_solution(1126280252515086938)
XLA Ops:
  0.0 0.0 copy-start
  0.0 1.2 %copy-done = bf16[1,32,2,8192]{3,2,1,0:T(2,128)(2,1)S(1)} copy-done((bf16[1,32,2,8192]{3,2,1,0:T(2,128)(2,1)S(1)}, bf16[1,32,2,8192]{3,2,1,0:T(2,128)(2,1)}, u32[]{:S(2)}) %copy-start) | copy-done | bytes 1048600
  1.2 0.0 copy-start.1
  1.2 0.7 %copy-done.1 = s32[32,32]{1,0:T(8,128)S(1)} copy-done((s32[32,32]{1,0:T(8,128)S(1)}, s32[32,32]{1,0:T(8,128)}, u32[]{:S(2)}) %copy-start.1) | copy-done | bytes 4120
  1.9 0.0 copy-start.2
  1.9 0.7 %copy-done.2 = s32[1,32]{1,0:T(1,128)S(1)} copy-done((s32[1,32]{1,0:T(1,128)S(1)}, s32[1,32]{1,0:T(1,128)}, u32[]{:S(2)}) %copy-start.2) | copy-done | bytes 152
  2.6 52.6 %shard_map.37 = f32[32,512]{1,0:T(8,128)S(1)} custom-call(bf16[1,32,2,8192]{3,2,1,0:T(2,128)(2,1)S(1)} %copy-done, s32[32,32]{1,0:T(8,128)S(1)} %copy-done.1, s32[1,32]{1,0:T(1,128)S(1)} %copy-done.2), custom_call_target="tpu_custom_call" | custom-call | flops 6000000000 | bytes 2000000 | tf_op jit(solution)/shard_map/pallas_call | solution.py:372
  55.2 0.6 %copy.5 = f32[2,16,512]{2,1,0:T(8,128)} copy(f32[2,16,512]{2,1,0:T(8,128)S(1)} %bitcast.1) | data formatting | bytes 131072
Async XLA Ops:
  0.0 1.2 %copy-start = (bf16[1,32,2,8192]{3,2,1,0:T(2,128)(2,1)S(1)}, bf16[1,32,2,8192]{3,2,1,0:T(2,128)(2,1)}, u32[]{:S(2)}) copy-start(bf16[1,32,2,8192]{3,2,1,0:T(2,128)(2,1)} %x_hbm.1) | copy-start | bytes 3145732
  1.2 0.7 %copy-start.1 = (s32[32,32]{1,0:T(8,128)S(1)}, s32[32,32]{1,0:T(8,128)}, u32[]{:S(2)}) copy-start(s32[32,32]{1,0:T(8,128)} %own_hbm.1) | copy-start | bytes 12292
  1.9 0.7 %copy-start.2 = (s32[1,32]{1,0:T(1,128)S(1)}, s32[1,32]{1,0:T(1,128)}, u32[]{:S(2)}) copy-start(s32[1,32]{1,0:T(1,128)} %avail_hbm.1) | copy-start | bytes 388

commit v6 on v4

--- a/solution.py
+++ b/solution.py
@@ -24,7 +24,7 @@
 STEPS = len(WIDTHS)
 STARTS = tuple(sum(WIDTHS[:s]) for s in range(STEPS))
 WIDEST = max(WIDTHS)
-AHEAD = 3
+AHEAD = 4
 PLANE = NX * N_WIN
 HALVES = 2
 QUAD = NZ // HALVES
@@ -307,8 +307,9 @@
     final_present[...] = availability_of(masks, own_ref[pl.ds(me_p, 1), :])
     for s in range(2, STEPS):
         relay(s)
-        process(s - 2)
-    for s in range(STEPS - 2, STEPS):
+        if s >= 4:
+            process(s - 4)
+    for s in range(STEPS - 4, STEPS):
         process(s)
 
     lag_send[...] = acc[...].astype(bf16).reshape(N_WIN, SHARE, LAGS)

time: 57.2 us -> 56.1 us (0.981)
  Pallas kernels: 53.8 us -> 52.7 us
    pallas_call x1, Pallas kernels: 53.8 us -> 52.7 us  [per_device(): pl.pallas_call(kernel, out_shape=jax.ShapeDtypeStruct((SHARE, LAGS), f32)...]
where the time goes in v6:
time: 56.1 us; the launch traced here: 55.9 us
  Pallas kernels  52.7 us (94%)
  local copies, waits for them, and re-layouts  3.23 us (6%)
    pallas_call x1, Pallas kernels, per_device(): pl.pallas_call(kernel, out_shape=jax.ShapeDtypeStruct((SHARE, LAGS), f32)...  52.7 us
    unnamed x7, local copies, waits for them, and re-layouts  3.23 us

profile of v6, /device:TPU:1, one launch (start us, length us, event | category | flops | bytes accessed | tf_op | source)
XLA Modules:
  0.0 55.9 jit_solution(5351834035713910447)
XLA Ops:
  0.0 0.0 copy-start
  0.0 1.2 %copy-done = bf16[1,32,2,8192]{3,2,1,0:T(2,128)(2,1)S(1)} copy-done((bf16[1,32,2,8192]{3,2,1,0:T(2,128)(2,1)S(1)}, bf16[1,32,2,8192]{3,2,1,0:T(2,128)(2,1)}, u32[]{:S(2)}) %copy-start) | copy-done | bytes 1048600
  1.2 0.0 copy-start.1
  1.2 0.7 %copy-done.1 = s32[32,32]{1,0:T(8,128)S(1)} copy-done((s32[32,32]{1,0:T(8,128)S(1)}, s32[32,32]{1,0:T(8,128)}, u32[]{:S(2)}) %copy-start.1) | copy-done | bytes 4120
  1.9 0.0 copy-start.2
  1.9 0.7 %copy-done.2 = s32[1,32]{1,0:T(1,128)S(1)} copy-done((s32[1,32]{1,0:T(1,128)S(1)}, s32[1,32]{1,0:T(1,128)}, u32[]{:S(2)}) %copy-start.2) | copy-done | bytes 152
  2.6 52.7 %shard_map.37 = f32[32,512]{1,0:T(8,128)S(1)} custom-call(bf16[1,32,2,8192]{3,2,1,0:T(2,128)(2,1)S(1)} %copy-done, s32[32,32]{1,0:T(8,128)S(1)} %copy-done.1, s32[1,32]{1,0:T(1,128)S(1)} %copy-done.2), custom_call_target="tpu_custom_call" | custom-call | flops 6000000000 | bytes 2000000 | tf_op jit(solution)/shard_map/pallas_call | solution.py:372
  55.3 0.6 %copy.5 = f32[2,16,512]{2,1,0:T(8,128)} copy(f32[2,16,512]{2,1,0:T(8,128)S(1)} %bitcast.1) | data formatting | bytes 131072
Async XLA Ops:
  0.0 1.2 %copy-start = (bf16[1,32,2,8192]{3,2,1,0:T(2,128)(2,1)S(1)}, bf16[1,32,2,8192]{3,2,1,0:T(2,128)(2,1)}, u32[]{:S(2)}) copy-start(bf16[1,32,2,8192]{3,2,1,0:T(2,128)(2,1)} %x_hbm.1) | copy-start | bytes 3145732
  1.2 0.7 %copy-start.1 = (s32[32,32]{1,0:T(8,128)S(1)}, s32[32,32]{1,0:T(8,128)}, u32[]{:S(2)}) copy-start(s32[32,32]{1,0:T(8,128)} %own_hbm.1) | copy-start | bytes 12292
  1.9 0.7 %copy-start.2 = (s32[1,32]{1,0:T(1,128)S(1)}, s32[1,32]{1,0:T(1,128)}, u32[]{:S(2)}) copy-start(s32[1,32]{1,0:T(1,128)} %avail_hbm.1) | copy-start | bytes 388

commit v7 on v6

--- a/solution.py
+++ b/solution.py
@@ -324,7 +324,7 @@
             device_id={"win": o, "pair": x * NZ + my_owner_z},
         )
 
-    for t in (4, 3, 5, 2, 6, 1, 7):
+    for t in (1, 7, 2, 6, 3, 5, 4):
         lagged(t).start()
 
     @pl.when(me_w == 1)

time: 56.1 us -> 56.5 us (level)
  no operation moved by 1% of the time
where the time goes in v7:
time: 56.5 us; the launch traced here: 55.8 us
  Pallas kernels  52.6 us (93%)
  local copies, waits for them, and re-layouts  3.23 us (6%)
    pallas_call x1, Pallas kernels, per_device(): pl.pallas_call(kernel, out_shape=jax.ShapeDtypeStruct((SHARE, LAGS), f32)...  52.6 us
    unnamed x7, local copies, waits for them, and re-layouts  3.23 us

profile of v7, /device:TPU:1, one launch (start us, length us, event | category | flops | bytes accessed | tf_op | source)
XLA Modules:
  0.0 55.8 jit_solution(6286395251586373047)
XLA Ops:
  0.0 0.0 copy-start
  0.0 1.2 %copy-done = bf16[1,32,2,8192]{3,2,1,0:T(2,128)(2,1)S(1)} copy-done((bf16[1,32,2,8192]{3,2,1,0:T(2,128)(2,1)S(1)}, bf16[1,32,2,8192]{3,2,1,0:T(2,128)(2,1)}, u32[]{:S(2)}) %copy-start) | copy-done | bytes 1048600
  1.2 0.0 copy-start.1
  1.2 0.7 %copy-done.1 = s32[32,32]{1,0:T(8,128)S(1)} copy-done((s32[32,32]{1,0:T(8,128)S(1)}, s32[32,32]{1,0:T(8,128)}, u32[]{:S(2)}) %copy-start.1) | copy-done | bytes 4120
  1.9 0.0 copy-start.2
  1.9 0.7 %copy-done.2 = s32[1,32]{1,0:T(1,128)S(1)} copy-done((s32[1,32]{1,0:T(1,128)S(1)}, s32[1,32]{1,0:T(1,128)}, u32[]{:S(2)}) %copy-start.2) | copy-done | bytes 152
  2.6 52.6 %shard_map.37 = f32[32,512]{1,0:T(8,128)S(1)} custom-call(bf16[1,32,2,8192]{3,2,1,0:T(2,128)(2,1)S(1)} %copy-done, s32[32,32]{1,0:T(8,128)S(1)} %copy-done.1, s32[1,32]{1,0:T(1,128)S(1)} %copy-done.2), custom_call_target="tpu_custom_call" | custom-call | flops 6000000000 | bytes 2000000 | tf_op jit(solution)/shard_map/pallas_call | solution.py:372
  55.2 0.6 %copy.5 = f32[2,16,512]{2,1,0:T(8,128)} copy(f32[2,16,512]{2,1,0:T(8,128)S(1)} %bitcast.1) | data formatting | bytes 131072
Async XLA Ops:
  0.0 1.2 %copy-start = (bf16[1,32,2,8192]{3,2,1,0:T(2,128)(2,1)S(1)}, bf16[1,32,2,8192]{3,2,1,0:T(2,128)(2,1)}, u32[]{:S(2)}) copy-start(bf16[1,32,2,8192]{3,2,1,0:T(2,128)(2,1)} %x_hbm.1) | copy-start | bytes 3145732
  1.2 0.7 %copy-start.1 = (s32[32,32]{1,0:T(8,128)S(1)}, s32[32,32]{1,0:T(8,128)}, u32[]{:S(2)}) copy-start(s32[32,32]{1,0:T(8,128)} %own_hbm.1) | copy-start | bytes 12292
  1.9 0.7 %copy-start.2 = (s32[1,32]{1,0:T(1,128)S(1)}, s32[1,32]{1,0:T(1,128)}, u32[]{:S(2)}) copy-start(s32[1,32]{1,0:T(1,128)} %avail_hbm.1) | copy-start | bytes 388
